TPU v7x, 256 devices: a whole 4x4x8 slice. The times are simulated.
256 devices in a mesh: node: 4 (over x), row: 16 (over z, core), col: 4 (over y).
Axes of the slice: x: 4, y: 4, z: 8, core: 2. Of those that a mesh axis runs over, the one named last changes fastest.
Arguments:
- basis_u: float32 [3, 64, 131072], P(None, 'col', ('node', 'row')), may hold values from -0.6 to 0.6
- basis_v: float32 [3, 64, 131072], P(None, 'col', ('node', 'row')), may hold values from -0.025 to 0.025
- leaf_diag: float32 [131072], P(('node', 'row')), may hold values from 1 to 4
- right_side: bfloat16 [1536, 131072], P('col', ('node', 'row')), may hold values from -6 to 6
- leaf_len: int32 [64], P(('node', 'row')), may hold values from 1 to 2048, 81920 in all
- ranks: int32 [3], replicated, may hold values from 32 to 64, as said below
Outputs:
- solution: float32 [1536, 131072], P('col', ('node', 'row'))
Inputs may be any that keep to these rules, and one draw needn't show every extreme that they name: `leaf_len`: some row block has all 2048 rows live. `ranks`: one level has rank 64.
All inputs are finite; a program needn't handle non-finite values.
Results may differ from a plain program's by a relative error of at most 0.0003.
Values sent between devices are 32-bit elements; how exact they have to be, the bound alone decides.
A program may use at most 64 MiB of HBM per device.

v0:
```python
import jax
import jax.numpy as jnp
from jax import lax
from jax.sharding import PartitionSpec as P

LEVELS = 3


def eliminate(matrix, rhs):
    size = matrix.shape[0]
    augmented = jnp.concatenate([matrix, rhs], axis=1)

    def step(index, augmented):
        pivot_row = lax.dynamic_slice_in_dim(augmented, index, 1, 0)
        pivot = lax.dynamic_slice_in_dim(pivot_row, index, 1, 1)
        pivot_row = pivot_row / pivot
        column = lax.dynamic_slice_in_dim(augmented, index, 1, 1)
        hit = jnp.arange(size)[:, None] == index
        return jnp.where(hit, pivot_row, augmented - column * pivot_row)

    augmented = lax.fori_loop(0, size, step, augmented)
    return augmented[:, size:]


def block_reduce(level, term):
    group = lax.axis_size("node") * lax.axis_size("row")
    place = lax.axis_index("node") * lax.axis_size("row") + lax.axis_index("row")
    span = group // (8 >> level)
    blocks = group // span
    block = place // span
    pick = (jnp.arange(blocks) == block).astype(jnp.float32)
    slotted = pick[:, None, None] * term[None]
    totals = lax.psum(slotted, ("node", "row"))
    own = lax.dynamic_index_in_dim(totals, block, 0, keepdims=False)
    sibling = lax.dynamic_index_in_dim(totals, jnp.bitwise_xor(block, 1), 0, keepdims=False)
    return (own, sibling)


def factor(panel, gram_own, gram_sib):
    high = lax.Precision.HIGHEST
    full_own, full_sib = (
        lax.all_gather(gram_own, "col", axis=1, tiled=True),
        lax.all_gather(gram_sib, "col", axis=1, tiled=True),
    )
    panel_full = lax.all_gather(panel, "col", axis=0, tiled=True)
    rank_all = full_own.shape[0]
    eye = jnp.eye(rank_all, dtype=jnp.float32)
    reduced = eye - jnp.dot(full_sib, full_own, precision=high)
    inverse = eliminate(reduced, eye)
    return (inverse, full_sib, panel_full)


def correct(factors, proj_own, proj_sib, target):
    high = lax.Precision.HIGHEST
    inverse, full_sib, panel_full = factors
    rhs = proj_sib - jnp.dot(full_sib, proj_own, precision=high)
    solved = jnp.dot(inverse, rhs, precision=high)
    return target - jnp.dot(solved.T, panel_full, precision=high)


def local(basis_u, basis_v, leaf_diag, right_side, leaf_len, ranks):
    high = lax.Precision.HIGHEST
    share = basis_u.shape[1]
    rows = basis_u.shape[2]
    live = (jnp.arange(rows) < leaf_len[0]).astype(jnp.float32)
    position = lax.axis_index("col") * share + jnp.arange(share)
    keep_share = (position[None, :] < ranks[:, None]).astype(jnp.float32)
    u_solved = basis_u * live[None, None, :] * keep_share[:, :, None] / leaf_diag[None, None, :]
    v_full = lax.all_gather(basis_v, "col", axis=1, tiled=True)
    rank_all = v_full.shape[1]
    keep_full = (jnp.arange(rank_all)[None, :] < ranks[:, None]).astype(jnp.float32)
    v_live = v_full * live[None, None, :] * keep_full[:, :, None]
    b_solved = right_side.astype(jnp.float32) / leaf_diag[None, :]
    panels = [u_solved[0], u_solved[1], u_solved[2]]
    current = b_solved
    for level in range(LEVELS):
        panel = panels[level]
        gram = jnp.dot(v_live[level], panel.T, precision=high)
        gram_own, gram_sib = block_reduce(level, gram)
        factors = factor(panel, gram_own, gram_sib)
        targets = panels[level + 1 :] + [current]
        results = []
        for target in targets:
            proj = jnp.dot(v_live[level], target.T, precision=high)
            proj_own, proj_sib = block_reduce(level, proj)
            results.append(correct(factors, proj_own, proj_sib, target))
        panels = panels[: level + 1] + results[:-1]
        current = results[-1]
    return current


def solution(mesh):
    in_specs = (
        P(None, "col", ("node", "row")),
        P(None, "col", ("node", "row")),
        P(("node", "row")),
        P("col", ("node", "row")),
        P(("node", "row")),
        P(),
    )
    out_specs = P("col", ("node", "row"))
    return jax.shard_map(local, mesh=mesh, in_specs=in_specs, out_specs=out_specs, check_vma=False)
```

profile of v0, /device:TPU:1, one launch (start us, length us, event | category | flops | bytes accessed | tf_op | source)
XLA Modules:
  0.0 1384.6 jit_solution(426167152795453995)
XLA Ops:
  10.0 12.6 all-gather.2
  22.6 19.5 %all-gather.9.cloned.1.call-done = f32[3,64,2048]{2,1,0:T(8,128)} async-done(((f32[3,16,2048]{2,1,0:T(8,128)}), f32[3,64,2048]{2,1,0:T(8,128)}) %all-gather.9.cloned.1.call-update) | async-done | bytes 1572880 | tf_op jit(solution)/shard_map/all_gather | solution.py:69
  45.7 3.1 fusion.3
  50.7 176.5 %all-reduce.13.cloned.1.call-done = (f32[8,64,16]{1,0,2:T(8,128)}, f32[8,64,16]{1,0,2:T(8,128)}, f32[8,64,16]{1,0,2:T(8,128)}) async-done(((f32[8,64,16]{1,0,2:T(8,128)}, f32[8,64,16]{1,0,2:T(8,128)}, f32[8,64,16]{1,0,2:T(8,128)}), (f32[8,64,16]{1,0,2:T(8,128)}, f32[8,64,16]{1,0,2:T(8,128)}, f32[8,64,16]{1,0,2:T(8,128)})) %all-reduce.13.cloned.1.call-update) | async-done | bytes 98320 | tf_op jit(solution)/shard_map/psum | solution.py:33
  228.1 9.4 all-gather
  237.5 9.0 all-gather.1
  246.9 93.9 %while.39 = (s32[]{:T(128)}, f32[64,128]{0,1:T(8,128)S(1)}, s32[]{:T(128)}, s32[]{:T(128)}, s32[]{:T(128)}, /*index=5*/s32[]{:T(128)}) while((s32[]{:T(128)}, f32[64,128]{0,1:T(8,128)S(1)}, s32[]{:T(128)}, s32[]{:T(128)}, s32[]{:T(128)}, /*index=5*/s32[]{:T(128)}) %tuple.94), condition=%wide.region_2.3_spmd, body=%wide.region_1.2_spmd.sunk | while | flops 24772 | bytes 68105 | solution.py:21
  343.0 10.5 all_gather.36
  354.8 250.5 %all-reduce = (f32[4,64,16]{1,0,2:T(4,128)S(1)}, f32[4,64,16]{1,0,2:T(4,128)S(1)}) all-reduce(f32[4,64,16]{1,0,2:T(4,128)S(1)} %get-tuple-element.203, f32[4,64,16]{1,0,2:T(4,128)S(1)} %get-tuple-element.202), channel_id=1, replica_groups=mesh['node'=4,'row'=16,'col'=4] {'node','row'}, use_global_device_ids=true, to_apply=%region_5.6 | all-reduce | flops 8192 | bytes 65536 | tf_op jit(solution)/shard_map/psum | solution.py:33
  605.3 9.3 all-gather.3
  614.5 9.0 all-gather.4
  624.0 93.9 %while.40 = (s32[]{:T(128)}, f32[64,128]{0,1:T(8,128)S(1)}, s32[]{:T(128)}, s32[]{:T(128)}, s32[]{:T(128)}, /*index=5*/s32[]{:T(128)}) while((s32[]{:T(128)}, f32[64,128]{0,1:T(8,128)S(1)}, s32[]{:T(128)}, s32[]{:T(128)}, s32[]{:T(128)}, /*index=5*/s32[]{:T(128)}) %tuple.97), condition=%wide.region_7.8_spmd, body=%wide.region_6.7_spmd.sunk | while | flops 24772 | bytes 68105 | solution.py:21
  719.1 251.7 %psum.70 = f32[2,64,16]{1,0,2:T(2,128)S(1)} all-reduce(f32[2,64,16]{1,0,2:T(2,128)S(1)} %broadcast_multiply_fusion.8), channel_id=1, replica_groups=mesh['node'=4,'row'=16,'col'=4] {'node','row'}, use_global_device_ids=true, to_apply=%region_11.12 | all-reduce | flops 2048 | bytes 16384 | tf_op jit(solution)/shard_map/psum | solution.py:33
  970.8 9.3 all-gather.5
  980.1 9.2 all-gather.6
  991.3 4.2 convolution_subtract_fusion.2
  995.6 3.1 fusion.11
  999.6 99.1 %while.41 = (s32[]{:T(128)}, f32[64,128]{0,1:T(8,128)S(1)}, s32[]{:T(128)}, s32[]{:T(128)}, s32[]{:T(128)}, /*index=5*/s32[]{:T(128)}) while((s32[]{:T(128)}, f32[64,128]{0,1:T(8,128)S(1)}, s32[]{:T(128)}, s32[]{:T(128)}, s32[]{:T(128)}, /*index=5*/s32[]{:T(128)}) %tuple.100), condition=%wide.region_13.14_spmd, body=%wide.region_12.13_spmd.sunk | while | flops 24772 | bytes 68105 | solution.py:21
  1098.8 84.0 %all-reduce.9.cloned.1.call-done = f32[4,64,384]{2,1,0:T(8,128)} async-done(((f32[4,64,384]{2,1,0:T(8,128)}), f32[4,64,384]{2,1,0:T(8,128)}) %all-reduce.9.cloned.1.call-update) | async-done | bytes 393232 | tf_op jit(solution)/shard_map/psum | solution.py:33
  1184.3 4.7 convolution_subtract_fusion.1
  1189.1 4.1 fusion.8
  1194.0 11.6 all_gather.39
  1205.5 165.6 %all-reduce.11.cloned.1.call-done = f32[2,64,384]{2,1,0:T(8,128)} async-done(((f32[2,64,384]{2,1,0:T(8,128)}), f32[2,64,384]{2,1,0:T(8,128)}) %all-reduce.11.cloned.1.call-update) | async-done | bytes 196624 | tf_op jit(solution)/shard_map/psum | solution.py:33
  1372.7 5.4 convolution_subtract_fusion
  (1035 shorter events, 298.6 us)
Async XLA Ops:
  6.5 16.0 %copy-start.4 = (s32[3]{0:T(128)S(1)}, s32[3]{0:T(128)}, u32[]{:S(2)}) copy-start(s32[3]{0:T(128)} %param.17) | copy-start | bytes 40
  6.5 35.6 %all-gather.9.cloned.1.call-start = ((), (), s32[]{:S(2)}) async-start(), calls=%async_computation | async-start | bytes 1966080 | tf_op jit(solution)/shard_map/all_gather | solution.py:69
  7.3 219.9 %all-reduce.13.cloned.1.call-start = ((), (), s32[]{:S(2)}) async-start(), calls=%async_computation.4 | async-start | bytes 393216 | tf_op jit(solution)/shard_map/psum | solution.py:33
  43.7 951.8 %copy-start = (f32[3,64,2048]{2,1,0:T(8,128)}, f32[3,64,2048]{2,1,0:T(8,128)S(1)}, u32[]{:S(2)}) copy-start(f32[3,64,2048]{2,1,0:T(8,128)S(1)} %multiply_multiply_fusion) | copy-start | bytes 4718596
  43.7 1.6 copy-start.3
  43.7 2.0 copy-start.5
  49.6 940.1 %all-reduce.7.cloned.1.call-start = ((), (), s32[]{:S(2)}) async-start(), calls=%async_computation.1 | async-start | bytes 1572864 | tf_op jit(solution)/shard_map/psum | solution.py:33
  50.7 1132.1 %all-reduce.9.cloned.1.call-start = ((), (), s32[]{:S(2)}) async-start(), calls=%async_computation.2 | async-start | bytes 786432 | tf_op jit(solution)/shard_map/psum | solution.py:33
  353.5 642.1 %copy-start.2 = (f32[64,2048]{1,0:T(8,128)}, f32[64,2048]{1,0:T(8,128)S(1)}, u32[]{:S(2)}) copy-start(f32[64,2048]{1,0:T(8,128)S(1)} %all_gather.36) | copy-start | bytes 1572868
  995.5 3.1 copy-start.1
  999.6 371.6 %all-reduce.11.cloned.1.call-start = ((), (), s32[]{:S(2)}) async-start(), calls=%async_computation.3 | async-start | bytes 393216 | tf_op jit(solution)/shard_map/psum | solution.py:33
Sparse Core Ops, SparseCore 0:
  9.2 32.8 all-gather.8
  49.7 177.4 all-reduce.12
  230.6 182.5 all-reduce.6
  999.7 183.0 all-reduce.8
  1194.1 177.0 all-reduce.10
where the time goes:
time: 1390 us; the launch traced here: 1380 us
  blocking collectives  592 us (43%)
  waiting for transfers between devices  446 us (32%)
  other arithmetic  170 us (12%)
  local copies, waits for them, and re-layouts  117 us (8%)
  matrix products  35 us (3%)
  between operations  14.2 us (1%)
    psum x2, blocking collectives, block_reduce(): totals = lax.psum(slotted, ('node', 'row'))  502 us
    psum x4, waiting for transfers between devices, block_reduce(): totals = lax.psum(slotted, ('node', 'row'))  426 us
    div x192, other arithmetic, step(): pivot_row = pivot_row / pivot  144 us
    dynamic_slice x192, local copies, waits for them, and re-layouts, step(): pivot = lax.dynamic_slice_in_dim(pivot_row, index, 1, 1)  113 us
    all_gather x3, blocking collectives, factor(): panel_full = lax.all_gather(panel, 'col', axis=0, tiled=True)  34.6 us
    all_gather x3, blocking collectives, factor(): lax.all_gather(gram_sib, 'col', axis=1, tiled=True)  27.9 us
  transfers between devices with their start and end apart: 5, of which 4 were waited for; matrix products, arithmetic and copies ran while one was open for 21% of the time, Pallas kernels for 0%

commit v1 on v0

v1 whole, which is shorter than its diff:
```python
import jax
import jax.numpy as jnp
from jax import lax
from jax.experimental import pallas as pl
from jax.experimental.pallas import tpu as pltpu
from jax.sharding import PartitionSpec as P

LEVELS = 3
ROWS = 2048
COLS = 384
MESH = pl.DeviceIdType.MESH


def mm(a, b):
    return jnp.dot(a, b, precision=lax.Precision.HIGHEST, preferred_element_type=jnp.float32)


def swap(a):
    return pltpu.roll(a, 64, 1)


def low_lanes(rows):
    return lax.broadcasted_iota(jnp.int32, (rows, 128), 1) < 64


def pick(low, high):
    return jnp.where(low_lanes(low.shape[0]), low, high)


def eye_pair():
    row = lax.broadcasted_iota(jnp.int32, (64, 128), 0)
    lane = lax.broadcasted_iota(jnp.int32, (64, 128), 1)
    return jnp.where((lane == row) | (lane == row + 64), 1.0, 0.0).astype(jnp.float32)


def invert(start):
    row8 = lax.broadcasted_iota(jnp.int32, (8, 128), 0)

    def body(_, carry):
        top, rest = carry
        for first in (0, 4):
            tops = [jnp.broadcast_to(top[:, j : j + 1], (8, 128)) for j in range(first, first + 4)]
            rests = [jnp.broadcast_to(rest[:, j : j + 1], (56, 128)) for j in range(first, first + 4)]
            for step in range(4):
                k = first + step
                hit = row8 == k
                scale = 1.0 / tops[step][k : k + 1, :]
                line = top[k : k + 1, :] * scale
                top = jnp.where(hit, line, top - tops[step] * line)
                rest = rest - rests[step] * line
                for j in range(step + 1, 4):
                    part = tops[j][k : k + 1, :] * scale
                    tops[j] = jnp.where(hit, part, tops[j] - tops[step] * part)
                    rests[j] = rests[j] - rests[step] * part
        whole = pltpu.roll(jnp.concatenate([rest, top], axis=0), 120, 1)
        return whole[0:8], whole[8:64]

    top, rest = lax.fori_loop(0, 8, body, (start[0:8], start[8:64]))
    whole = jnp.concatenate([top, rest], axis=0)
    return pick(whole, swap(whole))


def solve_kernel(
    ranks_ref, len_ref, diag_ref, v_ref, u_ref, b_ref,
    tt_ref, uall_ref,
    vall, ub, lhs, stage, pair, chip, zbuf, hybuf, x1src, x1buf, x2buf, agsrc, agbuf,
    loc_sem, v_s, v_r, u_s, u_r, d_s, d_r, z_s, z_r, h_s, h_r, x1_s, x1_r, x2_s, x2_r, ag_s, ag_r, ad_s, ad_r,
):
    x = lax.axis_index("node")
    row = lax.axis_index("row")
    y = lax.axis_index("col")
    z = row // 2
    h = row % 2
    idx = y * 2 + h
    right = (x, row, (y + 1) % 4)
    left = (x, row, (y + 3) % 4)
    ypast = (y + 3) % 4
    ynext = (y + 1) % 4
    partner = (x, z * 2 + (1 - h), y)
    xnear = x + 1 - 2 * (x % 2)
    xfar = 2 * (1 - x // 2)
    block = z // 4

    def z_peer(d):
        return (x, ((z + d) % 8) * 2 + h, y)

    def h_peer(d):
        other = (idx + d) % 8
        return (x, z * 2 + other % 2, other // 2)

    def x_peer(d):
        return ((x + d) % 4, row, y)

    peers = [z_peer(d) for d in range(1, 8)] + [h_peer(d) for d in range(1, 8)] + [x_peer(d) for d in range(1, 4)]
    barrier = pltpu.get_barrier_semaphore()
    for peer in peers:
        pl.semaphore_signal(barrier, inc=1, device_id=peer, device_id_type=MESH)
    pl.semaphore_wait(barrier, len(peers))

    def remote(src, dst, send, recv, device):
        return pltpu.make_async_remote_copy(
            src_ref=src, dst_ref=dst, send_sem=send, recv_sem=recv, device_id=device, device_id_type=MESH
        )

    sent = []

    def go(copy):
        copy.start()
        sent.append(copy)

    def direct(src, dst, send, recv, l):
        return (
            remote(src.at[l], dst.at[l, y], send.at[l, 0], recv.at[l, 0], right),
            remote(src.at[l], dst.at[l, y], send.at[l, 1], recv.at[l, 1], left),
        )

    def onward(dst, send, recv, l):
        return (
            remote(dst.at[l, ypast, 0], dst.at[l, ypast, 0], send.at[l, 2], recv.at[l, 2], right),
            remote(dst.at[l, ynext, 1], dst.at[l, ynext, 1], send.at[l, 3], recv.at[l, 3], left),
        )

    v_direct = [direct(v_ref, vall, v_s, v_r, l) for l in range(LEVELS)]
    v_onward = [onward(vall, v_s, v_r, l) for l in range(LEVELS)]
    u_direct = [direct(u_ref, uall_ref, u_s, u_r, l) for l in range(LEVELS)]
    u_onward = [onward(uall_ref, u_s, u_r, l) for l in range(LEVELS)]

    def send_direct(copies, l):
        for copy in copies[l]:
            go(copy)

    def pass_on(direct_copies, onward_copies, l):
        for copy in direct_copies[l]:
            copy.wait_recv()
        for copy in onward_copies[l]:
            go(copy)

    send_direct(v_direct, 0)
    own_v = pltpu.make_async_copy(v_ref, vall.at[:, y], loc_sem.at[0])
    own_u = pltpu.make_async_copy(u_ref, ub, loc_sem.at[1])
    own_b = pltpu.make_async_copy(b_ref, lhs.at[0:COLS], loc_sem.at[2])
    keep_u = pltpu.make_async_copy(u_ref, uall_ref.at[:, y], loc_sem.at[3])
    own_v.start()
    own_u.start()
    own_b.start()
    keep_u.start()
    send_direct(v_direct, 1)

    weight = jnp.where(
        lax.broadcasted_iota(jnp.int32, (1, ROWS), 1) < len_ref[0], 1.0 / diag_ref[...], 0.0
    )
    own_u.wait()
    eight = lax.broadcasted_iota(jnp.int32, (8, 1), 0)
    parts = []
    for half in range(2):
        for l in range(LEVELS):
            kept = jnp.where(y * 16 + half * 8 + eight < ranks_ref[l], 1.0, 0.0)
            parts.append(ub[l, half] * kept)
    mine = jnp.concatenate(parts, axis=0)
    mine_hi = mine.astype(jnp.bfloat16)
    lhs[COLS : COLS + 48] = mine_hi
    lhs[COLS + 48 : COLS + 96] = (mine - mine_hi.astype(jnp.float32)).astype(jnp.bfloat16)
    own_v.wait()
    own_b.wait()

    def product(l):
        for copy in v_onward[l]:
            copy.wait_recv()
        kept = jnp.where(lax.broadcasted_iota(jnp.int32, (64, 1), 0) < ranks_ref[l], 1.0, 0.0)
        total = None
        for part in range(4):
            span = slice(512 * part, 512 * part + 512)
            scaled = vall[l, :, :, :, span].reshape(64, 512) * weight[:, span] * kept
            high = scaled.astype(jnp.bfloat16)
            low = (scaled - high.astype(jnp.float32)).astype(jnp.bfloat16)
            both = jnp.concatenate([high, low], axis=0)
            term = lax.dot_general(
                lhs[:, span], both, (((1,), (1,)), ((), ())), preferred_element_type=jnp.float32
            )
            total = term if total is None else total + term
        from_b = total[0:COLS]
        from_b = (from_b + swap(from_b)).reshape(2, 8, 24, 128)
        from_u = total[COLS : COLS + 48] + total[COLS + 48 : COLS + 96]
        from_u = (from_u + swap(from_u)).reshape(2, 1, 24, 128)
        lanes = lax.broadcasted_iota(jnp.int32, (2, 8, 24, 128), 3) < 64
        stage[l] = jnp.where(lanes, from_b, from_u)

    d_copies = [remote(stage.at[l, 1 - h], pair.at[l], d_s.at[l], d_r.at[l], partner) for l in range(LEVELS)]
    z_copies = [
        [remote(chip.at[l, (z + d) % 8], zbuf.at[l, z], z_s.at[l, d], z_r.at[l, d], z_peer(d)) for d in range(1, 8)]
        for l in range(LEVELS)
    ]
    h_copies = [
        [remote(hybuf.at[l, idx], hybuf.at[l, idx], h_s.at[l, d], h_r.at[l, d], h_peer(d)) for d in range(1, 8)]
        for l in range(LEVELS)
    ]

    def send_z(l):
        d_copies[l].wait_recv()
        chip[l] = stage[l, h] + pair[l]
        for copy in z_copies[l]:
            go(copy)
        zbuf[l, z] = chip[l, z]

    def send_h(l):
        for copy in z_copies[l]:
            copy.wait_recv()
        first = (zbuf[l, 0] + zbuf[l, 1]) + (zbuf[l, 2] + zbuf[l, 3])
        second = (zbuf[l, 4] + zbuf[l, 5]) + (zbuf[l, 6] + zbuf[l, 7])
        hybuf[l, idx] = pick(swap(first), second)
        for copy in h_copies[l]:
            go(copy)
        return pick(first, swap(second))

    def gathered(l, from_b):
        for copy in h_copies[l]:
            copy.wait_recv()
        panels = [hybuf[l, :, 8 * k : 8 * k + 8].reshape(64, 128) for k in range(LEVELS)]
        return panels[0], jnp.concatenate([panels[1], panels[2], from_b], axis=0)

    pass_on(v_direct, v_onward, 0)
    send_direct(v_direct, 2)
    product(0)
    go(d_copies[0])
    pass_on(v_direct, v_onward, 1)
    send_z(0)
    product(1)
    go(d_copies[1])
    b_0 = send_h(0)
    pass_on(v_direct, v_onward, 2)
    for l in range(LEVELS):
        send_direct(u_direct, l)
    send_z(1)

    panel, rhs = gathered(0, b_0)
    turned = swap(panel)
    inverse = invert(eye_pair() - mm(panel[:, :64], jnp.where(low_lanes(64), turned, 0.0)))

    product(2)
    go(d_copies[2])
    b_1 = send_h(1)
    send_z(2)

    rhs_turned = swap(rhs)
    first = mm(rhs_turned[:, :64] - mm(rhs[:, :64], turned[:, :64]), inverse)
    second = rhs_turned - mm(first[:, :64], pick(panel, turned))
    t0 = pick(first, second)

    def after_zero(l, from_b):
        lead, raw = gathered(l, from_b)
        lead_turned = swap(lead)
        stacked = jnp.concatenate([pick(lead, lead_turned), pick(lead_turned, lead)], axis=0)
        return raw + swap(raw) - mm(t0, stacked)

    w1 = after_zero(1, b_1)
    x1src[0:64] = pick(w1[0:64], w1[64:128])
    x1src[64:88] = w1[128:152]
    x1_copy = remote(x1src, x1buf, x1_s.at[0], x1_r.at[0], (xnear, row, y))
    go(x1_copy)
    b_2 = send_h(2)
    x1_copy.wait_recv()
    sib_panel = x1buf[0:64]
    sib_rhs = jnp.concatenate([swap(sib_panel), x1buf[64:88]], axis=0)
    inverse = invert(eye_pair() - mm(w1[0:64, :64], jnp.where(low_lanes(64), sib_panel, 0.0)))
    t1 = mm(sib_rhs[:, :64] - mm(w1[64:152, :64], sib_panel[:, :64]), inverse)

    agsrc[0] = pick(t0[128:152], t1[64:88])
    agsrc[1] = pick(swap(t0[128:152]), t1[64:88])
    ag0 = [
        remote(agsrc.at[((z + d) % 8) // 4], agbuf.at[0, h, z], ag_s.at[0, d], ag_r.at[0, d], z_peer(d))
        for d in range(1, 8)
    ]
    for copy in ag0:
        go(copy)
    agbuf[0, h, z] = agsrc[block]

    pass_on(u_direct, u_onward, 0)

    w2 = after_zero(2, b_2)
    x2buf[x] = w2[64:152] - mm(t1[:, :64], w2[0:64])
    x2_copies = [remote(x2buf.at[x], x2buf.at[x], x2_s.at[d], x2_r.at[d], x_peer(d)) for d in range(1, 4)]
    for copy in x2_copies:
        go(copy)
    for copy in ag0:
        copy.wait_recv()
    ad0 = remote(agbuf.at[0, h], agbuf.at[0, h], ad_s.at[0], ad_r.at[0], partner)
    go(ad0)
    pass_on(u_direct, u_onward, 1)
    for copy in x2_copies:
        copy.wait_recv()
    own = x2buf[x] + x2buf[xnear]
    sib = x2buf[xfar] + x2buf[xfar + 1]
    inverse = invert(eye_pair() - mm(own[0:64, :64], jnp.where(low_lanes(64), sib[0:64], 0.0)))
    t2 = mm(sib[64:88, :64] - mm(own[64:88, :64], sib[0:64, :64]), inverse)
    agbuf[1, h, z] = t2
    ag1 = [
        remote(agbuf.at[1, h, z], agbuf.at[1, h, z], ag_s.at[1, d], ag_r.at[1, d], z_peer(d)) for d in range(1, 8)
    ]
    for copy in ag1:
        go(copy)
    pass_on(u_direct, u_onward, 2)
    for copy in ag1:
        copy.wait_recv()
    ad1 = remote(agbuf.at[1, h], agbuf.at[1, h], ad_s.at[1], ad_r.at[1], partner)
    go(ad1)
    ad0.wait_recv()
    ad1.wait_recv()

    early = agbuf[0].reshape(COLS, 128)
    late = agbuf[1].reshape(COLS, 128)
    a_0 = jnp.where(block == 0, t0[0:128], swap(t0[0:128]))
    a_0 = pick(a_0, swap(a_0))
    c_1 = pick(swap(early), early) - mm(late[:, :64], t1[0:64])
    c_0 = early - mm(pick(c_1, late), a_0)
    lane = lax.broadcasted_iota(jnp.int32, (1, 128), 1)
    keep_01 = jnp.where(lane < jnp.where(lane < 64, ranks_ref[0], 64 + ranks_ref[1]), 1.0, 0.0)
    keep_2 = jnp.where(lane < ranks_ref[2], 1.0, 0.0)
    tt_ref[:, 0:128] = pick(c_0, c_1) * keep_01
    tt_ref[:, 128:256] = late * keep_2

    for l in range(LEVELS):
        for copy in u_onward[l]:
            copy.wait_recv()
    keep_u.wait()
    for copy in sent:
        copy.wait_send()


def final_kernel(width, len_ref, tt_ref, u_ref, b_ref, diag_ref, out_ref):
    coef = tt_ref[:, 0:192]
    coef_hi = coef.astype(jnp.bfloat16)
    coef_lo = (coef - coef_hi.astype(jnp.float32)).astype(jnp.bfloat16)
    panel = u_ref[...]
    panel_hi = panel.astype(jnp.bfloat16)
    panel_lo = (panel - panel_hi.astype(jnp.float32)).astype(jnp.bfloat16)

    def dot(a, b):
        return jnp.dot(a, b, preferred_element_type=jnp.float32)

    total = dot(coef_hi, panel_hi) + (dot(coef_lo, panel_hi) + dot(coef_hi, panel_lo))
    place = pl.program_id(0) * width + lax.broadcasted_iota(jnp.int32, (1, width), 1)
    live = place < len_ref[0]
    out_ref[...] = (b_ref[...].astype(jnp.float32) - jnp.where(live, total, 0.0)) * (1.0 / diag_ref[...])


def local(basis_u, basis_v, leaf_diag, right_side, leaf_len, ranks):
    f32 = jnp.float32
    diag = leaf_diag.reshape(1, ROWS)
    smem = pl.BlockSpec(memory_space=pltpu.SMEM)
    vmem = pl.BlockSpec(memory_space=pltpu.VMEM)
    hbm = pl.BlockSpec(memory_space=pl.ANY)
    dma = pltpu.SemaphoreType.DMA
    coef, panels = pl.pallas_call(
        solve_kernel,
        name="gather_and_solve",
        out_shape=(
            jax.ShapeDtypeStruct((COLS, 256), f32),
            jax.ShapeDtypeStruct((LEVELS, 4, 2, 8, ROWS), f32),
        ),
        in_specs=[smem, smem, vmem, hbm, hbm, hbm],
        out_specs=(vmem, hbm),
        scratch_shapes=[
            pltpu.VMEM((LEVELS, 4, 2, 8, ROWS), f32),
            pltpu.VMEM((LEVELS, 2, 8, ROWS), f32),
            pltpu.VMEM((COLS + 96, ROWS), jnp.bfloat16),
            pltpu.VMEM((LEVELS, 2, 8, 24, 128), f32),
            pltpu.VMEM((LEVELS, 8, 24, 128), f32),
            pltpu.VMEM((LEVELS, 8, 24, 128), f32),
            pltpu.VMEM((LEVELS, 8, 24, 128), f32),
            pltpu.VMEM((LEVELS, 8, 24, 128), f32),
            pltpu.VMEM((88, 128), f32),
            pltpu.VMEM((88, 128), f32),
            pltpu.VMEM((4, 88, 128), f32),
            pltpu.VMEM((2, 24, 128), f32),
            pltpu.VMEM((2, 2, 8, 24, 128), f32),
            dma((4,)),
            dma((LEVELS, 4)), dma((LEVELS, 4)),
            dma((LEVELS, 4)), dma((LEVELS, 4)),
            dma((LEVELS,)), dma((LEVELS,)),
            dma((LEVELS, 8)), dma((LEVELS, 8)),
            dma((LEVELS, 8)), dma((LEVELS, 8)),
            dma((1,)), dma((1,)),
            dma((4,)), dma((4,)),
            dma((2, 8)), dma((2, 8)),
            dma((2,)), dma((2,)),
        ],
        compiler_params=pltpu.CompilerParams(
            collective_id=0, has_side_effects=True, vmem_limit_bytes=32 * 1024 * 1024
        ),
    )(
        ranks,
        leaf_len,
        diag,
        basis_v.reshape(LEVELS, 2, 8, ROWS),
        basis_u.reshape(LEVELS, 2, 8, ROWS),
        right_side,
    )
    width = 512
    return pl.pallas_call(
        lambda *refs: final_kernel(width, *refs),
        name="correct_rows",
        grid=(ROWS // width,),
        out_shape=jax.ShapeDtypeStruct((COLS, ROWS), f32),
        in_specs=[
            smem,
            pl.BlockSpec((COLS, 256), lambda i: (0, 0)),
            pl.BlockSpec((192, width), lambda i: (0, i)),
            pl.BlockSpec((COLS, width), lambda i: (0, i)),
            pl.BlockSpec((1, width), lambda i: (0, i)),
        ],
        out_specs=pl.BlockSpec((COLS, width), lambda i: (0, i)),
        compiler_params=pltpu.CompilerParams(vmem_limit_bytes=32 * 1024 * 1024),
        cost_estimate=pl.CostEstimate(flops=2 * 3 * COLS * 192 * ROWS, bytes_accessed=6300000, transcendentals=0),
    )(leaf_len, coef, panels.reshape(192, ROWS), right_side, diag)


def solution(mesh):
    in_specs = (
        P(None, "col", ("node", "row")),
        P(None, "col", ("node", "row")),
        P(("node", "row")),
        P("col", ("node", "row")),
        P(("node", "row")),
        P(),
    )
    out_specs = P("col", ("node", "row"))
    return jax.shard_map(local, mesh=mesh, in_specs=in_specs, out_specs=out_specs, check_vma=False)
```

time: 1390 us -> 76.4 us (0.05)
  blocking collectives: 592 us -> 0 us
  waiting for transfers between devices: 446 us -> 0 us
  other arithmetic: 170 us -> 0 us
  local copies, waits for them, and re-layouts: 117 us -> 4.75 us
  Pallas kernels: 0 us -> 70.7 us
  matrix products: 35 us -> 0 us
    psum x2 -> x0, blocking collectives: 502 us -> none  [block_reduce(): totals = lax.psum(slotted, ('node', 'row'))]
    psum x4 -> x0, waiting for transfers between devices: 426 us -> none  [block_reduce(): totals = lax.psum(slotted, ('node', 'row'))]
    div x193 -> x0, other arithmetic: 145 us -> none  [the longest x192 144 us: step(): pivot_row = pivot_row / pivot]
    dynamic_slice x197 -> x0, local copies, waits for them, and re-layouts: 115 us -> none  [the longest x192 113 us: step(): pivot = lax.dynamic_slice_in_dim(pivot_row, index, 1, 1)]
    all_gather x9 -> x0, blocking collectives: 89.8 us -> none  [the longest x3 34.6 us: factor(): panel_full = lax.all_gather(panel, 'col', axis=0, tiled=True)]
    pallas_call x0 -> x2, Pallas kernels: none -> 70.7 us  [the longest x1 67.3 us: local(): pl.pallas_call(solve_kernel, name='gather_and_solve', out_shape=(jax.Shap...]
    dot_general x30 -> x0, matrix products: 35.1 us -> none  [the longest x6 15.5 us: correct(): return target - jnp.dot(solved.T, panel_full, precision=high)]
    all_gather x1 -> x0, waiting for transfers between devices: 19.5 us -> none  [local(): v_full = lax.all_gather(basis_v, 'col', axis=1, tiled=True)]
  transfers between devices with their start and end apart: 5 -> 0, of which waited for: 4 -> 0; matrix products, arithmetic and copies ran while one was open for 21% -> 0% of each run, Pallas kernels for 0% -> 0%
where the time goes in v1:
time: 76.4 us; the launch traced here: 76.1 us
  Pallas kernels  70.7 us (93%)
  local copies, waits for them, and re-layouts  4.75 us (6%)
    pallas_call x1, Pallas kernels, local(): pl.pallas_call(solve_kernel, name='gather_and_solve', out_shape=(jax.Shap...  67.3 us
    unnamed x12, local copies, waits for them, and re-layouts  4.75 us
    pallas_call x1, Pallas kernels, local(): pl.pallas_call(lambda *refs: final_kernel(width, *refs), name='correct_ro...  3.42 us

profile of v1, /device:TPU:1, one launch (start us, length us, event | category | flops | bytes accessed | tf_op | source)
XLA Modules:
  0.0 76.1 jit_solution(3975873897168228113)
XLA Ops:
  0.7 0.0 copy-start
  0.7 1.4 %copy-done = bf16[384,2048]{1,0:T(8,128)(2,1)S(1)} copy-done((bf16[384,2048]{1,0:T(8,128)(2,1)S(1)}, bf16[384,2048]{1,0:T(8,128)(2,1)}, u32[]{:S(2)}) %copy-start) | copy-done | bytes 1572888
  2.1 0.0 copy-start.2
  2.1 1.0 %copy-done.2 = f32[3,16,2048]{2,1,0:T(8,128)S(1)} copy-done((f32[3,16,2048]{2,1,0:T(8,128)S(1)}, f32[3,16,2048]{2,1,0:T(8,128)}, u32[]{:S(2)}) %copy-start.2) | copy-done | bytes 393240
  3.1 0.0 copy-start.3
  3.1 1.0 %copy-done.3 = f32[3,16,2048]{2,1,0:T(8,128)S(1)} copy-done((f32[3,16,2048]{2,1,0:T(8,128)S(1)}, f32[3,16,2048]{2,1,0:T(8,128)}, u32[]{:S(2)}) %copy-start.3) | copy-done | bytes 393240
  4.1 0.0 copy-start.4
  4.1 0.7 copy-done.4
  4.8 0.0 copy-start.5
  4.8 0.7 copy-done.5
  5.4 0.0 copy-start.1
  5.4 67.3 %gather_and_solve.1 = (f32[384,256]{1,0:T(8,128)S(1)}, f32[3,4,2,8,2048]{4,3,2,1,0:T(8,128)S(1)}) custom-call(s32[3]{0:T(128)S(1)} %copy-done.5, s32[1]{0:T(128)S(6)} %copy.7.len_ref.refs_0_, f32[1,2048]{1,0:T(1,128)S(1)} %bitcast.7, f32[3,2,8,2048]{3,2,1,0:T(8,128)S(1)} %bitcast.5, f32[3,2,8,2048]{3,2,1,0:T(8,128)S(1)} %bitcast.6, bf16[384,2048]{1,0:T(8,128)(2,1)S(1)} %copy-done), custom_call_target="tpu_custom_call" | custom-call | tf_op jit(solution)/shard_map/gather_and_solve/pallas_call | solution.py:353
  72.7 0.0 copy-done.1
  72.7 3.4 %correct_rows.1 = f32[384,2048]{1,0:T(8,128)} custom-call(s32[1]{0:T(128)S(6)} %copy.7.len_ref.refs_0_, f32[384,256]{1,0:T(8,128)S(1)} %get-tuple-element.7.refs_1_, f32[192,2048]{1,0:T(8,128)S(1)} %bitcast.4, bf16[384,2048]{1,0:T(8,128)(2,1)S(1)} %copy-done.1, f32[1,2048]{1,0:T(1,128)S(1)} %bitcast.8), custom_call_target="tpu_custom_call" | custom-call | flops 905969664 | bytes 6300000 | tf_op jit(solution)/shard_map/correct_rows/pallas_call | solution.py:399
Async XLA Ops:
  0.7 1.4 %copy-start = (bf16[384,2048]{1,0:T(8,128)(2,1)S(1)}, bf16[384,2048]{1,0:T(8,128)(2,1)}, u32[]{:S(2)}) copy-start(bf16[384,2048]{1,0:T(8,128)(2,1)} %refs_3_.1) | copy-start | bytes 4718596
  2.1 1.0 %copy-start.2 = (f32[3,16,2048]{2,1,0:T(8,128)S(1)}, f32[3,16,2048]{2,1,0:T(8,128)}, u32[]{:S(2)}) copy-start(f32[3,16,2048]{2,1,0:T(8,128)} %param.7) | copy-start | bytes 1179652
  3.1 1.0 %copy-start.3 = (f32[3,16,2048]{2,1,0:T(8,128)S(1)}, f32[3,16,2048]{2,1,0:T(8,128)}, u32[]{:S(2)}) copy-start(f32[3,16,2048]{2,1,0:T(8,128)} %param.6) | copy-start | bytes 1179652
  4.1 0.7 copy-start.4
  4.8 0.7 copy-start.5
  5.4 67.3 %copy-start.1 = (bf16[384,2048]{1,0:T(8,128)(2,1)S(1)}, bf16[384,2048]{1,0:T(8,128)(2,1)}, u32[]{:S(2)}) copy-start(bf16[384,2048]{1,0:T(8,128)(2,1)} %refs_3_.1) | copy-start | bytes 4718596

commit v2 on v1

v2 whole, which is shorter than its diff:
```python
import jax
import jax.numpy as jnp
from jax import lax
from jax.experimental import pallas as pl
from jax.experimental.pallas import tpu as pltpu
from jax.sharding import PartitionSpec as P

LEVELS = 3
ROWS = 2048
COLS = 384
MESH = pl.DeviceIdType.MESH


def split(a):
    high = a.astype(jnp.bfloat16)
    return high, (a - high.astype(jnp.float32)).astype(jnp.bfloat16)


def dot(a, b):
    return jnp.dot(a, b, preferred_element_type=jnp.float32)


def mm(a, b):
    high = a.astype(jnp.bfloat16).astype(jnp.float32)
    parts = pick(high, a - high).astype(jnp.bfloat16)
    left = jnp.concatenate([parts, high.astype(jnp.bfloat16)[:, :64]], axis=1)
    b_high, b_low = split(b)
    return dot(left, jnp.concatenate([b_high, b_high, b_low], axis=0))


def swap(a):
    return pltpu.roll(a, 64, 1)


def low_lanes(rows):
    return lax.broadcasted_iota(jnp.int32, (rows, 128), 1) < 64


def pick(low, high):
    return jnp.where(low_lanes(low.shape[0]), low, high)


def eye_pair():
    row = lax.broadcasted_iota(jnp.int32, (64, 128), 0)
    lane = lax.broadcasted_iota(jnp.int32, (64, 128), 1)
    return jnp.where((lane == row) | (lane == row + 64), 1.0, 0.0).astype(jnp.float32)


def invert(starts):
    row8 = lax.broadcasted_iota(jnp.int32, (8, 128), 0)

    def eight_steps(top, rest):
        for first in (0, 4):
            tops = [jnp.broadcast_to(top[:, j : j + 1], (8, 128)) for j in range(first, first + 4)]
            rests = [jnp.broadcast_to(rest[:, j : j + 1], (56, 128)) for j in range(first, first + 4)]
            for step in range(4):
                k = first + step
                hit = row8 == k
                scale = 1.0 / tops[step][k : k + 1, :]
                line = top[k : k + 1, :] * scale
                top = jnp.where(hit, line, top - tops[step] * line)
                rest = rest - rests[step] * line
                for j in range(step + 1, 4):
                    part = tops[j][k : k + 1, :] * scale
                    tops[j] = jnp.where(hit, part, tops[j] - tops[step] * part)
                    rests[j] = rests[j] - rests[step] * part
        whole = pltpu.roll(jnp.concatenate([rest, top], axis=0), 120, 1)
        return whole[0:8], whole[8:64]

    def body(_, carry):
        return tuple(eight_steps(*one) for one in carry)

    done = lax.fori_loop(0, 8, body, tuple((start[0:8], start[8:64]) for start in starts))
    wholes = [jnp.concatenate(one, axis=0) for one in done]
    return [pick(whole, swap(whole)) for whole in wholes]


def both(a):
    turned = swap(a)
    return pick(a, turned), pick(turned, a)


def eye_less(product):
    return eye_pair() - jnp.where(low_lanes(64), product, 0.0)


def solve_kernel(
    len_ref, ranks_in, diag_in, v_ref, u_ref, b_ref,
    sum_ref, left_ref, right_ref,
    ranks_ref, diag_ref, uall_ref, vall, lhs, stage, pair, chip, zbuf, ubuf, bbuf, agsrc, couple, first_t, second_t, early, late,
    loc_sem, v_s, v_r, u_s, u_r, d_s, d_r, z_s, z_r, h_s, h_r, b_s, b_r, e_s, e_r, ag_s, ag_r, ad_s, ad_r,
):
    x = lax.axis_index("node")
    row = lax.axis_index("row")
    y = lax.axis_index("col")
    own_v = pltpu.make_async_copy(v_ref, vall.at[:, y], loc_sem.at[0])
    own_u = pltpu.make_async_copy(u_ref, uall_ref.at[:, y], loc_sem.at[1])
    own_b = pltpu.make_async_copy(b_ref, lhs.at[0:COLS], loc_sem.at[2])
    small = [
        pltpu.make_async_copy(src, dst, loc_sem.at[3 + i])
        for i, (src, dst) in enumerate(((ranks_in, ranks_ref), (diag_in, diag_ref)))
    ]
    for copy in small + [own_u, own_v, own_b]:
        copy.start()
    z = row // 2
    h = row % 2
    right = (x, row, (y + 1) % 4)
    left = (x, row, (y + 3) % 4)
    ypast = (y + 3) % 4
    ynext = (y + 1) % 4
    partner = (x, z * 2 + (1 - h), y)
    block = z // 4

    def z_peer(d):
        return (x, ((z + d) % 8) * 2 + h, y)

    def plane_peer(d):
        return ((x + d // 4) % 4, row, (y + d % 4) % 4)

    peers = [partner] + [z_peer(d) for d in range(1, 8)] + [plane_peer(d) for d in range(1, 16)]
    barrier = pltpu.get_barrier_semaphore()
    for peer in peers:
        pl.semaphore_signal(barrier, inc=1, device_id=peer, device_id_type=MESH)
    pl.semaphore_wait(barrier, len(peers))

    def remote(src, dst, send, recv, device):
        return pltpu.make_async_remote_copy(
            src_ref=src, dst_ref=dst, send_sem=send, recv_sem=recv, device_id=device, device_id_type=MESH
        )

    sent = []

    def go(copy):
        copy.start()
        sent.append(copy)

    def direct(src, dst, send, recv, l):
        return (
            remote(src.at[l], dst.at[l, y], send.at[l, 0], recv.at[l, 0], right),
            remote(src.at[l], dst.at[l, y], send.at[l, 1], recv.at[l, 1], left),
        )

    def onward(dst, send, recv, l):
        return (
            remote(dst.at[l, ypast, 0], dst.at[l, ypast, 0], send.at[l, 2], recv.at[l, 2], right),
            remote(dst.at[l, ynext, 1], dst.at[l, ynext, 1], send.at[l, 3], recv.at[l, 3], left),
        )

    v_direct = [direct(v_ref, vall, v_s, v_r, l) for l in range(LEVELS)]
    v_onward = [onward(vall, v_s, v_r, l) for l in range(LEVELS)]
    u_direct = [direct(u_ref, uall_ref, u_s, u_r, l) for l in range(LEVELS)]
    u_onward = [onward(uall_ref, u_s, u_r, l) for l in range(LEVELS)]

    def send_direct(copies, l):
        for copy in copies[l]:
            go(copy)

    def pass_on(direct_copies, onward_copies, l):
        for copy in direct_copies[l]:
            copy.wait_recv()
        for copy in onward_copies[l]:
            go(copy)

    send_direct(v_direct, 0)
    send_direct(v_direct, 1)
    for copy in small:
        copy.wait()

    over = 1.0 / diag_ref[...]
    weight = jnp.where(lax.broadcasted_iota(jnp.int32, (1, ROWS), 1) < len_ref[0], over, 0.0)
    own_u.wait()
    eight = lax.broadcasted_iota(jnp.int32, (8, 1), 0)
    parts = []
    for half in range(2):
        for l in range(LEVELS):
            kept = jnp.where(y * 16 + half * 8 + eight < ranks_ref[l], 1.0, 0.0)
            parts.append(uall_ref[l, y, half] * kept)
    mine = jnp.concatenate(parts, axis=0)
    mine_hi = mine.astype(jnp.bfloat16)
    lhs[COLS : COLS + 48] = mine_hi
    lhs[COLS + 48 : COLS + 96] = (mine - mine_hi.astype(jnp.float32)).astype(jnp.bfloat16)
    own_v.wait()
    own_b.wait()

    def product(l):
        for copy in v_onward[l]:
            copy.wait_recv()
        kept = jnp.where(lax.broadcasted_iota(jnp.int32, (64, 1), 0) < ranks_ref[l], 1.0, 0.0)
        total = None
        for part in range(4):
            span = slice(512 * part, 512 * part + 512)
            scaled = vall[l, :, :, :, span].reshape(64, 512) * weight[:, span] * kept
            high = scaled.astype(jnp.bfloat16)
            low = (scaled - high.astype(jnp.float32)).astype(jnp.bfloat16)
            both = jnp.concatenate([high, low], axis=0)
            term = lax.dot_general(
                lhs[:, span], both, (((1,), (1,)), ((), ())), preferred_element_type=jnp.float32
            )
            total = term if total is None else total + term
        from_b = total[0:COLS]
        from_b = (from_b + swap(from_b)).reshape(2, 8, 24, 128)
        from_u = total[COLS : COLS + 48] + total[COLS + 48 : COLS + 96]
        from_u = (from_u + swap(from_u)).reshape(2, 1, 24, 128)
        lanes = lax.broadcasted_iota(jnp.int32, (2, 8, 24, 128), 3) < 64
        stage[l] = jnp.where(lanes, from_b, from_u)

    d_copies = [remote(stage.at[l, 1 - h], pair.at[l], d_s.at[l], d_r.at[l], partner) for l in range(LEVELS)]
    z_copies = [
        [remote(chip.at[l, (z + d) % 8], zbuf.at[l, z], z_s.at[l, d], z_r.at[l, d], z_peer(d)) for d in range(1, 8)]
        for l in range(LEVELS)
    ]
    plane_copies = [
        [
            remote(ubuf.at[l, h, x, y], ubuf.at[l, h, x, y], h_s.at[l, d], h_r.at[l, d], plane_peer(d))
            for d in range(1, 16)
        ]
        + [
            remote(bbuf.at[l, x], bbuf.at[l, x], b_s.at[l, d], b_r.at[l, d], plane_peer(4 * d))
            for d in range(1, 4)
        ]
        for l in range(LEVELS)
    ]
    share_copies = [remote(ubuf.at[l, h], ubuf.at[l, h], e_s.at[l], e_r.at[l], partner) for l in range(LEVELS)]

    def send_z(l):
        d_copies[l].wait_recv()
        chip[l] = stage[l, h] + pair[l]
        for copy in z_copies[l]:
            go(copy)
        zbuf[l, z] = chip[l, z]

    def send_plane(l):
        for copy in z_copies[l]:
            copy.wait_recv()
        first = (zbuf[l, 0] + zbuf[l, 1]) + (zbuf[l, 2] + zbuf[l, 3])
        second = (zbuf[l, 4] + zbuf[l, 5]) + (zbuf[l, 6] + zbuf[l, 7])
        ubuf[l, h, x, y] = pick(swap(first), second)
        bbuf[l, x] = pick(first, swap(second))
        for copy in plane_copies[l]:
            go(copy)

    def share(l):
        for copy in plane_copies[l]:
            copy.wait_recv()
        go(share_copies[l])

    def gathered(l, at):
        panels = [
            jnp.concatenate(
                [ubuf[l, half, at, col, 8 * k : 8 * k + 8] for col in range(4) for half in range(2)], axis=0
            )
            for k in range(LEVELS)
        ]
        return panels[0], jnp.concatenate([panels[1], panels[2], bbuf[l, at]], axis=0)

    pass_on(v_direct, v_onward, 0)
    send_direct(v_direct, 2)
    pass_on(v_direct, v_onward, 1)
    product(0)
    go(d_copies[0])
    send_z(0)
    pass_on(v_direct, v_onward, 2)
    product(1)
    go(d_copies[1])
    send_z(1)
    product(2)
    go(d_copies[2])
    send_z(2)
    send_plane(0)
    send_plane(1)
    share(0)
    send_plane(2)
    for l in range(LEVELS):
        send_direct(u_direct, l)
    share_copies[0].wait_recv()

    zero = [[both(part) for part in gathered(0, at)] for at in range(4)]
    inverse = invert([eye_less(mm(panel[0], panel[1])) for panel, _ in zero])
    share(1)
    t_low, t_high = [], []
    for at in range(4):
        (g_low, g_high), (q_low, q_high) = zero[at]
        t_low.append(mm(q_high - mm(q_low, g_high), inverse[at]))
        t_high.append(q_low - mm(t_low[at], g_low))
        first_t[at, 0] = t_low[at][0:128]
        first_t[at, 1] = t_high[at][0:128]
    share_copies[1].wait_recv()

    def after_zero(l, at):
        lead, raw = gathered(l, at)
        n_low, n_high = both(lead)
        return raw + swap(raw) - (mm(t_low[at], n_low) + mm(t_high[at], n_high))

    w1 = [after_zero(1, at) for at in range(4)]
    for at in range(4):
        sides = pick(w1[at // 2 * 2][128:152], w1[at // 2 * 2 + 1][128:152])
        for c, t in ((0, t_low[at]), (1, t_high[at])):
            agsrc[at, c, 0:24] = t[128:152]
            agsrc[at, c, 24:48] = sides
    early_copies = [
        remote(agsrc.at[x, ((z + d) % 8) // 4], early.at[h, z], ag_s.at[0, d], ag_r.at[0, d], z_peer(d))
        for d in range(1, 8)
    ]
    for copy in early_copies:
        go(copy)
    early[h, z] = agsrc[x, block]
    inverse = invert([eye_less(mm(w1[at][0:64], w1[at + 1][0:64])) for at in (0, 2)])
    share(2)
    pass_on(u_direct, u_onward, 0)
    t1 = []
    for even in (0, 2):
        low, high = w1[even], w1[even + 1]
        one = mm(high[64:152] - mm(low[64:152], high[0:64]), inverse[even // 2])
        t1 += [one, low[64:152] - mm(one, low[0:64])]
        couple[even // 2, 0] = low[0:64]
        couple[even // 2, 1] = high[0:64]
        couple[even // 2, 2] = inverse[even // 2]
    for at in range(4):
        second_t[at] = t1[at][0:64]
    share_copies[2].wait_recv()

    w2 = [after_zero(2, at) for at in range(4)]
    p2 = [w2[at][64:152] - mm(t1[at], w2[at][0:64]) for at in range(4)]
    low, high = p2[0] + p2[1], p2[2] + p2[3]
    own = jnp.where(x < 2, low, high)
    sib = jnp.where(x < 2, high, low)
    late[h, z] = pick(own[64:88], sib[64:88])
    late_copies = [
        remote(late.at[h, z], late.at[h, z], ag_s.at[1, d], ag_r.at[1, d], z_peer(d)) for d in range(1, 8)
    ]
    for copy in late_copies:
        go(copy)
    pass_on(u_direct, u_onward, 1)
    pass_on(u_direct, u_onward, 2)
    (inverse,) = invert([eye_less(mm(own[0:64], sib[0:64]))])
    for copy in early_copies:
        copy.wait_recv()
    early_share = remote(early.at[h], early.at[h], ad_s.at[0], ad_r.at[0], partner)
    go(early_share)

    a_01 = first_t[x, block, 0:64]
    a_02 = first_t[x, block, 64:128]
    a_12 = second_t[x]
    c_1 = mm(inverse, a_12)
    c_0 = mm(inverse, a_02) - mm(c_1, a_01)
    last_01 = -pick(c_0, c_1)
    last_2 = inverse[:, :64]
    early_share.wait_recv()
    t_0 = early[:, :, 0:24].reshape(COLS, 128)
    q_even, q_odd = both(early[:, :, 24:48].reshape(COLS, 128))
    t_even = mm(q_odd - mm(q_even, couple[x // 2, 1]), couple[x // 2, 2])
    t_odd = q_even - mm(t_even, couple[x // 2, 0])
    t_1 = jnp.where(x % 2 == 0, t_even, t_odd)
    t_0 = t_0 - mm(t_1, a_01)
    front_high, front_low = split(pick(t_0, t_1))
    last_high, last_low = split(jnp.concatenate([last_01, last_2], axis=1))
    for l in range(LEVELS):
        for copy in u_onward[l]:
            copy.wait_recv()
    place = lax.broadcasted_iota(jnp.int32, (64, 1), 0)
    kept = jnp.concatenate([jnp.where(place < ranks_ref[l], 1.0, 0.0) for l in range(LEVELS)], axis=0)
    for part in range(4):
        span = slice(512 * part, 512 * part + 512)
        panel_high, panel_low = split(uall_ref[:, :, :, :, span].reshape(192, 512) * kept)
        last = dot(last_high, panel_high) + (dot(last_low, panel_high) + dot(last_high, panel_low))
        last_h, last_l = split(last * weight[:, span])
        right_ref[0:64, span] = last_h
        right_ref[64:128, span] = last_h
        right_ref[128:192, span] = last_l
        front = dot(front_high, panel_high[0:128]) + (
            dot(front_low, panel_high[0:128]) + dot(front_high, panel_low[0:128])
        )
        sum_ref[:, span] = lhs[0:COLS, span].astype(jnp.float32) * over[:, span] - front * weight[:, span]

    for copy in late_copies:
        copy.wait_recv()
    late_share = remote(late.at[h], late.at[h], ad_s.at[1], ad_r.at[1], partner)
    go(late_share)
    late_share.wait_recv()
    q_own, q_sib = both(late[...].reshape(COLS, 128))
    rest = q_sib - mm(q_own, sib[0:64])
    rest_high = rest.astype(jnp.bfloat16).astype(jnp.float32)
    left_ref[:, 0:128] = pick(rest_high, rest - rest_high).astype(jnp.bfloat16)
    left_ref[:, 128:192] = rest_high.astype(jnp.bfloat16)[:, :64]

    for copy in sent:
        copy.wait_send()


def final_kernel(sum_ref, left_ref, right_ref, out_ref):
    out_ref[...] = sum_ref[...] - dot(left_ref[...], right_ref[...])


def local(basis_u, basis_v, leaf_diag, right_side, leaf_len, ranks):
    f32 = jnp.float32
    diag = leaf_diag.reshape(1, ROWS)
    vmem = pl.BlockSpec(memory_space=pltpu.VMEM)
    dma = pltpu.SemaphoreType.DMA
    total, left, right = pl.pallas_call(
        solve_kernel,
        name="gather_and_solve",
        out_shape=(
            pltpu.VMEM((COLS, ROWS), f32),
            pltpu.VMEM((COLS, 192), jnp.bfloat16),
            pltpu.VMEM((192, ROWS), jnp.bfloat16),
        ),
        in_specs=[pl.BlockSpec(memory_space=pltpu.SMEM)] + [pl.BlockSpec(memory_space=pltpu.HBM)] * 5,
        out_specs=(vmem, vmem, vmem),
        scratch_shapes=[
            pltpu.SMEM((LEVELS,), jnp.int32),
            pltpu.VMEM((1, ROWS), f32),
            pltpu.VMEM((LEVELS, 4, 2, 8, ROWS), f32),
            pltpu.VMEM((LEVELS, 4, 2, 8, ROWS), f32),
            pltpu.VMEM((COLS + 96, ROWS), jnp.bfloat16),
            pltpu.VMEM((LEVELS, 2, 8, 24, 128), f32),
            pltpu.VMEM((LEVELS, 8, 24, 128), f32),
            pltpu.VMEM((LEVELS, 8, 24, 128), f32),
            pltpu.VMEM((LEVELS, 8, 24, 128), f32),
            pltpu.VMEM((LEVELS, 2, 4, 4, 24, 128), f32),
            pltpu.VMEM((LEVELS, 4, 24, 128), f32),
            pltpu.VMEM((4, 2, 48, 128), f32),
            pltpu.VMEM((2, 3, 64, 128), f32),
            pltpu.VMEM((4, 2, 128, 128), f32),
            pltpu.VMEM((4, 64, 128), f32),
            pltpu.VMEM((2, 8, 48, 128), f32),
            pltpu.VMEM((2, 8, 24, 128), f32),
            dma((5,)),
            dma((LEVELS, 4)), dma((LEVELS, 4)),
            dma((LEVELS, 4)), dma((LEVELS, 4)),
            dma((LEVELS,)), dma((LEVELS,)),
            dma((LEVELS, 8)), dma((LEVELS, 8)),
            dma((LEVELS, 16)), dma((LEVELS, 16)),
            dma((LEVELS, 4)), dma((LEVELS, 4)),
            dma((LEVELS,)), dma((LEVELS,)),
            dma((2, 8)), dma((2, 8)),
            dma((2,)), dma((2,)),
        ],
        compiler_params=pltpu.CompilerParams(
            collective_id=0, has_side_effects=True, vmem_limit_bytes=40 * 1024 * 1024
        ),
    )(
        leaf_len,
        *[
            pltpu.with_memory_space_constraint(array, pltpu.HBM)
            for array in (
                ranks,
                diag,
                basis_v.reshape(LEVELS, 2, 8, ROWS),
                basis_u.reshape(LEVELS, 2, 8, ROWS),
                right_side,
            )
        ]
    )
    width = 512
    return pl.pallas_call(
        final_kernel,
        name="add_last_panel",
        grid=(ROWS // width,),
        out_shape=jax.ShapeDtypeStruct((COLS, ROWS), f32),
        in_specs=[
            pl.BlockSpec((COLS, width), lambda i: (0, i)),
            pl.BlockSpec((COLS, 192), lambda i: (0, 0)),
            pl.BlockSpec((192, width), lambda i: (0, i)),
        ],
        out_specs=pl.BlockSpec((COLS, width), lambda i: (0, i)),
        compiler_params=pltpu.CompilerParams(vmem_limit_bytes=32 * 1024 * 1024),
        cost_estimate=pl.CostEstimate(flops=2 * COLS * 192 * ROWS, bytes_accessed=7200000, transcendentals=0),
    )(total, left, right)


def solution(mesh):
    in_specs = (
        P(None, "col", ("node", "row")),
        P(None, "col", ("node", "row")),
        P(("node", "row")),
        P("col", ("node", "row")),
        P(("node", "row")),
        P(),
    )
    out_specs = P("col", ("node", "row"))
    return jax.shard_map(local, mesh=mesh, in_specs=in_specs, out_specs=out_specs, check_vma=False)
```

time: 76.4 us -> 67 us (0.88)
  local copies, waits for them, and re-layouts: 4.75 us -> 0 us
  Pallas kernels: 70.7 us -> 66.2 us
    unnamed x12 -> x0, local copies, waits for them, and re-layouts: 4.75 us -> none
    pallas_call x2, Pallas kernels: 70.7 us -> 66.2 us  [the longest x1 63.4 us: local(): pl.pallas_call(solve_kernel, name='gather_and_solve', out_shape=(pltpu.VM...]
where the time goes in v2:
time: 67 us; the launch traced here: 66.9 us
  Pallas kernels  66.2 us (99%)
    pallas_call x1, Pallas kernels, local(): pl.pallas_call(solve_kernel, name='gather_and_solve', out_shape=(pltpu.VM...  63.4 us
    pallas_call x1, Pallas kernels, local(): pl.pallas_call(final_kernel, name='add_last_panel', grid=(ROWS // width,)...  2.77 us

profile of v2, /device:TPU:1, one launch (start us, length us, event | category | flops | bytes accessed | tf_op | source)
XLA Modules:
  0.0 66.9 jit_solution(17583203378612418367)
XLA Ops:
  0.7 63.4 %gather_and_solve.1 = (f32[384,2048]{1,0:T(8,128)S(1)}, bf16[384,192]{1,0:T(8,128)(2,1)S(1)}, bf16[192,2048]{1,0:T(8,128)(2,1)S(1)}) custom-call(s32[1]{0:T(128)S(6)} %copy.7.len_ref, s32[3]{0:T(128)} %ranks_in.1, f32[1,2048]{1,0:T(1,128)} %bitcast.5, f32[3,2,8,2048]{3,2,1,0:T(8,128)} %bitcast.3, f32[3,2,8,2048]{3,2,1,0:T(8,128)} %bitcast.4, ...), custom_call_target="tpu_custom_call" | custom-call | tf_op jit(solution)/shard_map/gather_and_solve/pallas_call | solution.py:399
  64.1 2.8 %add_last_panel.1 = f32[384,2048]{1,0:T(8,128)} custom-call(f32[384,2048]{1,0:T(8,128)S(1)} %get-tuple-element.8.sum_ref, bf16[384,192]{1,0:T(8,128)(2,1)S(1)} %get-tuple-element.9.left_ref, bf16[192,2048]{1,0:T(8,128)(2,1)S(1)} %get-tuple-element.10.right_ref), custom_call_target="tpu_custom_call" | custom-call | flops 301989888 | bytes 7200000 | tf_op jit(solution)/shard_map/add_last_panel/pallas_call | solution.py:455

commit v3 on v2

--- a/solution.py
+++ b/solution.py
@@ -1,3 +1,5 @@
+import functools
+
 import jax
 import jax.numpy as jnp
 from jax import lax
@@ -114,58 +116,18 @@
     def z_peer(d):
         return (x, ((z + d) % 8) * 2 + h, y)
 
+    def core_peer(d):
+        return (x, (row + d) % 16, y)
+
     def plane_peer(d):
         return ((x + d // 4) % 4, row, (y + d % 4) % 4)
 
-    peers = [partner] + [z_peer(d) for d in range(1, 8)] + [plane_peer(d) for d in range(1, 16)]
+    peers = [core_peer(d) for d in range(1, 16)] + [plane_peer(d) for d in range(1, 16)]
     barrier = pltpu.get_barrier_semaphore()
     for peer in peers:
         pl.semaphore_signal(barrier, inc=1, device_id=peer, device_id_type=MESH)
-    pl.semaphore_wait(barrier, len(peers))
-
-    def remote(src, dst, send, recv, device):
-        return pltpu.make_async_remote_copy(
-            src_ref=src, dst_ref=dst, send_sem=send, recv_sem=recv, device_id=device, device_id_type=MESH
-        )
-
-    sent = []
-
-    def go(copy):
-        copy.start()
-        sent.append(copy)
-
-    def direct(src, dst, send, recv, l):
-        return (
-            remote(src.at[l], dst.at[l, y], send.at[l, 0], recv.at[l, 0], right),
-            remote(src.at[l], dst.at[l, y], send.at[l, 1], recv.at[l, 1], left),
-        )
-
-    def onward(dst, send, recv, l):
-        return (
-            remote(dst.at[l, ypast, 0], dst.at[l, ypast, 0], send.at[l, 2], recv.at[l, 2], right),
-            remote(dst.at[l, ynext, 1], dst.at[l, ynext, 1], send.at[l, 3], recv.at[l, 3], left),
-        )
-
-    v_direct = [direct(v_ref, vall, v_s, v_r, l) for l in range(LEVELS)]
-    v_onward = [onward(vall, v_s, v_r, l) for l in range(LEVELS)]
-    u_direct = [direct(u_ref, uall_ref, u_s, u_r, l) for l in range(LEVELS)]
-    u_onward = [onward(uall_ref, u_s, u_r, l) for l in range(LEVELS)]
-
-    def send_direct(copies, l):
-        for copy in copies[l]:
-            go(copy)
-
-    def pass_on(direct_copies, onward_copies, l):
-        for copy in direct_copies[l]:
-            copy.wait_recv()
-        for copy in onward_copies[l]:
-            go(copy)
-
-    send_direct(v_direct, 0)
-    send_direct(v_direct, 1)
     for copy in small:
         copy.wait()
-
     over = 1.0 / diag_ref[...]
     weight = jnp.where(lax.broadcasted_iota(jnp.int32, (1, ROWS), 1) < len_ref[0], over, 0.0)
     own_u.wait()
@@ -179,6 +141,55 @@
     mine_hi = mine.astype(jnp.bfloat16)
     lhs[COLS : COLS + 48] = mine_hi
     lhs[COLS + 48 : COLS + 96] = (mine - mine_hi.astype(jnp.float32)).astype(jnp.bfloat16)
+    pl.semaphore_wait(barrier, len(peers))
+
+    def remote(src, dst, send, recv, device):
+        return pltpu.make_async_remote_copy(
+            src_ref=src, dst_ref=dst, send_sem=send, recv_sem=recv, device_id=device, device_id_type=MESH
+        )
+
+    sent = []
+
+    def go(copy):
+        copy.start()
+        sent.append(copy)
+
+    def start_all(copies):
+        for copy in copies:
+            copy.start()
+
+    def wait_all(whole, sem):
+        pltpu.make_async_copy(whole, whole, sem).wait()
+
+    def direct(src, dst, send, recv, l):
+        return (
+            remote(src.at[l], dst.at[l, y], send.at[l, 0], recv.at[l, 0], right),
+            remote(src.at[l], dst.at[l, y], send.at[l, 1], recv.at[l, 1], left),
+        )
+
+    def onward(dst, send, recv, l):
+        return (
+            remote(dst.at[l, ypast, 0], dst.at[l, ypast, 0], send.at[l, 2], recv.at[l, 2], right),
+            remote(dst.at[l, ynext, 1], dst.at[l, ynext, 1], send.at[l, 3], recv.at[l, 3], left),
+        )
+
+    v_direct = [direct(v_ref, vall, v_s, v_r, l) for l in range(LEVELS)]
+    v_onward = [onward(vall, v_s, v_r, l) for l in range(LEVELS)]
+    u_direct = [direct(u_ref, uall_ref, u_s, u_r, l) for l in range(LEVELS)]
+    u_onward = [onward(uall_ref, u_s, u_r, l) for l in range(LEVELS)]
+
+    def send_direct(copies, l):
+        for copy in copies[l]:
+            go(copy)
+
+    def pass_on(direct_copies, onward_copies, l):
+        for copy in direct_copies[l]:
+            copy.wait_recv()
+        for copy in onward_copies[l]:
+            go(copy)
+
+    send_direct(v_direct, 0)
+    send_direct(v_direct, 1)
     own_v.wait()
     own_b.wait()
 
@@ -206,18 +217,16 @@
 
     d_copies = [remote(stage.at[l, 1 - h], pair.at[l], d_s.at[l], d_r.at[l], partner) for l in range(LEVELS)]
     z_copies = [
-        [remote(chip.at[l, (z + d) % 8], zbuf.at[l, z], z_s.at[l, d], z_r.at[l, d], z_peer(d)) for d in range(1, 8)]
+        [remote(chip.at[l, (z + d) % 8], zbuf.at[l, z], z_s.at[l], z_r.at[l], z_peer(d)) for d in range(1, 8)]
         for l in range(LEVELS)
     ]
-    plane_copies = [
-        [
-            remote(ubuf.at[l, h, x, y], ubuf.at[l, h, x, y], h_s.at[l, d], h_r.at[l, d], plane_peer(d))
-            for d in range(1, 16)
-        ]
-        + [
-            remote(bbuf.at[l, x], bbuf.at[l, x], b_s.at[l, d], b_r.at[l, d], plane_peer(4 * d))
-            for d in range(1, 4)
-        ]
+    spot = x * 4 + y
+    u_copies = [
+        [remote(ubuf.at[l, h, spot], ubuf.at[l, h, spot], h_s.at[l], h_r.at[l], plane_peer(d)) for d in range(1, 16)]
+        for l in range(LEVELS)
+    ]
+    b_copies = [
+        [remote(bbuf.at[l, x], bbuf.at[l, x], b_s.at[l], b_r.at[l], plane_peer(4 * d)) for d in range(1, 4)]
         for l in range(LEVELS)
     ]
     share_copies = [remote(ubuf.at[l, h], ubuf.at[l, h], e_s.at[l], e_r.at[l], partner) for l in range(LEVELS)]
@@ -225,29 +234,27 @@
     def send_z(l):
         d_copies[l].wait_recv()
         chip[l] = stage[l, h] + pair[l]
-        for copy in z_copies[l]:
-            go(copy)
+        start_all(z_copies[l])
         zbuf[l, z] = chip[l, z]
 
     def send_plane(l):
-        for copy in z_copies[l]:
-            copy.wait_recv()
+        wait_all(zbuf.at[l, 0:7], z_r.at[l])
         first = (zbuf[l, 0] + zbuf[l, 1]) + (zbuf[l, 2] + zbuf[l, 3])
         second = (zbuf[l, 4] + zbuf[l, 5]) + (zbuf[l, 6] + zbuf[l, 7])
-        ubuf[l, h, x, y] = pick(swap(first), second)
+        ubuf[l, h, spot] = pick(swap(first), second)
         bbuf[l, x] = pick(first, swap(second))
-        for copy in plane_copies[l]:
-            go(copy)
+        start_all(u_copies[l])
+        start_all(b_copies[l])
 
     def share(l):
-        for copy in plane_copies[l]:
-            copy.wait_recv()
+        wait_all(ubuf.at[l, h, 0:15], h_r.at[l])
+        wait_all(bbuf.at[l, 0:3], b_r.at[l])
         go(share_copies[l])
 
     def gathered(l, at):
         panels = [
             jnp.concatenate(
-                [ubuf[l, half, at, col, 8 * k : 8 * k + 8] for col in range(4) for half in range(2)], axis=0
+                [ubuf[l, half, 4 * at + col, 8 * k : 8 * k + 8] for col in range(4) for half in range(2)], axis=0
             )
             for k in range(LEVELS)
         ]
@@ -298,11 +305,10 @@
             agsrc[at, c, 0:24] = t[128:152]
             agsrc[at, c, 24:48] = sides
     early_copies = [
-        remote(agsrc.at[x, ((z + d) % 8) // 4], early.at[h, z], ag_s.at[0, d], ag_r.at[0, d], z_peer(d))
+        remote(agsrc.at[x, ((z + d) % 8) // 4], early.at[h, z], ag_s.at[0], ag_r.at[0], z_peer(d))
         for d in range(1, 8)
     ]
-    for copy in early_copies:
-        go(copy)
+    start_all(early_copies)
     early[h, z] = agsrc[x, block]
     inverse = invert([eye_less(mm(w1[at][0:64], w1[at + 1][0:64])) for at in (0, 2)])
     share(2)
@@ -324,17 +330,15 @@
     low, high = p2[0] + p2[1], p2[2] + p2[3]
     own = jnp.where(x < 2, low, high)
     sib = jnp.where(x < 2, high, low)
-    late[h, z] = pick(own[64:88], sib[64:88])
+    late[h * 8 + z] = pick(own[64:88], sib[64:88])
     late_copies = [
-        remote(late.at[h, z], late.at[h, z], ag_s.at[1, d], ag_r.at[1, d], z_peer(d)) for d in range(1, 8)
-    ]
-    for copy in late_copies:
-        go(copy)
+        remote(late.at[h * 8 + z], late.at[h * 8 + z], ag_s.at[1], ag_r.at[1], core_peer(d)) for d in range(1, 16)
+    ]
+    start_all(late_copies)
     pass_on(u_direct, u_onward, 1)
     pass_on(u_direct, u_onward, 2)
     (inverse,) = invert([eye_less(mm(own[0:64], sib[0:64]))])
-    for copy in early_copies:
-        copy.wait_recv()
+    wait_all(early.at[h, 0:7], ag_r.at[0])
     early_share = remote(early.at[h], early.at[h], ad_s.at[0], ad_r.at[0], partner)
     go(early_share)
 
@@ -372,23 +376,26 @@
         )
         sum_ref[:, span] = lhs[0:COLS, span].astype(jnp.float32) * over[:, span] - front * weight[:, span]
 
-    for copy in late_copies:
-        copy.wait_recv()
-    late_share = remote(late.at[h], late.at[h], ad_s.at[1], ad_r.at[1], partner)
-    go(late_share)
-    late_share.wait_recv()
+    for copy in sent:
+        copy.wait_send()
+    for l in range(LEVELS):
+        wait_all(chip.at[l, 0:7], z_s.at[l])
+        wait_all(ubuf.at[l, h, 0:15], h_s.at[l])
+        wait_all(bbuf.at[l, 0:3], b_s.at[l])
+    wait_all(early.at[h, 0:7], ag_s.at[0])
+    wait_all(late.at[0:15], ag_r.at[1])
     q_own, q_sib = both(late[...].reshape(COLS, 128))
     rest = q_sib - mm(q_own, sib[0:64])
     rest_high = rest.astype(jnp.bfloat16).astype(jnp.float32)
     left_ref[:, 0:128] = pick(rest_high, rest - rest_high).astype(jnp.bfloat16)
     left_ref[:, 128:192] = rest_high.astype(jnp.bfloat16)[:, :64]
 
-    for copy in sent:
-        copy.wait_send()
-
-
-def final_kernel(sum_ref, left_ref, right_ref, out_ref):
-    out_ref[...] = sum_ref[...] - dot(left_ref[...], right_ref[...])
+    wait_all(late.at[0:15], ag_s.at[1])
+
+
+def final_kernel(width, sum_ref, left_ref, right_ref, out_ref):
+    span = pl.ds(pl.multiple_of(pl.program_id(0) * width, width), width)
+    out_ref[...] = sum_ref[:, span] - dot(left_ref[...], right_ref[:, span])
 
 
 def local(basis_u, basis_v, leaf_diag, right_side, leaf_len, ranks):
@@ -416,24 +423,24 @@
             pltpu.VMEM((LEVELS, 8, 24, 128), f32),
             pltpu.VMEM((LEVELS, 8, 24, 128), f32),
             pltpu.VMEM((LEVELS, 8, 24, 128), f32),
-            pltpu.VMEM((LEVELS, 2, 4, 4, 24, 128), f32),
+            pltpu.VMEM((LEVELS, 2, 16, 24, 128), f32),
             pltpu.VMEM((LEVELS, 4, 24, 128), f32),
             pltpu.VMEM((4, 2, 48, 128), f32),
             pltpu.VMEM((2, 3, 64, 128), f32),
             pltpu.VMEM((4, 2, 128, 128), f32),
             pltpu.VMEM((4, 64, 128), f32),
             pltpu.VMEM((2, 8, 48, 128), f32),
-            pltpu.VMEM((2, 8, 24, 128), f32),
+            pltpu.VMEM((16, 24, 128), f32),
             dma((5,)),
             dma((LEVELS, 4)), dma((LEVELS, 4)),
             dma((LEVELS, 4)), dma((LEVELS, 4)),
             dma((LEVELS,)), dma((LEVELS,)),
-            dma((LEVELS, 8)), dma((LEVELS, 8)),
-            dma((LEVELS, 16)), dma((LEVELS, 16)),
-            dma((LEVELS, 4)), dma((LEVELS, 4)),
             dma((LEVELS,)), dma((LEVELS,)),
-            dma((2, 8)), dma((2, 8)),
+            dma((LEVELS,)), dma((LEVELS,)),
+            dma((LEVELS,)), dma((LEVELS,)),
+            dma((LEVELS,)), dma((LEVELS,)),
             dma((2,)), dma((2,)),
+            dma((1,)), dma((1,)),
         ],
         compiler_params=pltpu.CompilerParams(
             collective_id=0, has_side_effects=True, vmem_limit_bytes=40 * 1024 * 1024
@@ -453,15 +460,11 @@
     )
     width = 512
     return pl.pallas_call(
-        final_kernel,
+        functools.partial(final_kernel, width),
         name="add_last_panel",
         grid=(ROWS // width,),
         out_shape=jax.ShapeDtypeStruct((COLS, ROWS), f32),
-        in_specs=[
-            pl.BlockSpec((COLS, width), lambda i: (0, i)),
-            pl.BlockSpec((COLS, 192), lambda i: (0, 0)),
-            pl.BlockSpec((192, width), lambda i: (0, i)),
-        ],
+        in_specs=[vmem, vmem, vmem],
         out_specs=pl.BlockSpec((COLS, width), lambda i: (0, i)),
         compiler_params=pltpu.CompilerParams(vmem_limit_bytes=32 * 1024 * 1024),
         cost_estimate=pl.CostEstimate(flops=2 * COLS * 192 * ROWS, bytes_accessed=7200000, transcendentals=0),

time: 67 us -> 63.7 us (0.951)
  Pallas kernels: 66.2 us -> 62.9 us
    pallas_call x1, Pallas kernels: 63.4 us -> 60.3 us  [local(): pl.pallas_call(solve_kernel, name='gather_and_solve', out_shape=(pltpu.VM...]
where the time goes in v3:
time: 63.7 us; the launch traced here: 63.6 us
  Pallas kernels  62.9 us (99%)
  between operations  0.66 us (1%)
    pallas_call x1, Pallas kernels, local(): pl.pallas_call(solve_kernel, name='gather_and_solve', out_shape=(pltpu.VM...  60.3 us
    pallas_call x1, Pallas kernels, local(): pl.pallas_call(functools.partial(final_kernel, width), name='add_last_pan...  2.58 us

profile of v3, /device:TPU:1, one launch (start us, length us, event | category | flops | bytes accessed | tf_op | source)
XLA Modules:
  0.0 63.6 jit_solution(7629416486365181304)
XLA Ops:
  0.7 60.3 %gather_and_solve.1 = (f32[384,2048]{1,0:T(8,128)S(1)}, bf16[384,192]{1,0:T(8,128)(2,1)S(1)}, bf16[192,2048]{1,0:T(8,128)(2,1)S(1)}) custom-call(s32[1]{0:T(128)S(6)} %copy.7.len_ref, s32[3]{0:T(128)} %ranks_in.1, f32[1,2048]{1,0:T(1,128)} %bitcast.5, f32[3,2,8,2048]{3,2,1,0:T(8,128)} %bitcast.3, f32[3,2,8,2048]{3,2,1,0:T(8,128)} %bitcast.4, ...), custom_call_target="tpu_custom_call" | custom-call | tf_op jit(solution)/shard_map/gather_and_solve/pallas_call | solution.py:406
  61.0 2.6 %add_last_panel.1 = f32[384,2048]{1,0:T(8,128)} custom-call(f32[384,2048]{1,0:T(8,128)S(1)} %get-tuple-element.8.sum_ref, bf16[384,192]{1,0:T(8,128)(2,1)S(1)} %get-tuple-element.9.left_ref, bf16[192,2048]{1,0:T(8,128)(2,1)S(1)} %get-tuple-element.10.right_ref), custom_call_target="tpu_custom_call" | custom-call | flops 301989888 | bytes 7200000 | tf_op jit(solution)/shard_map/add_last_panel/pallas_call | solution.py:462

commit v4 on v3

--- a/solution.py
+++ b/solution.py
@@ -42,39 +42,63 @@
     return jnp.where(low_lanes(low.shape[0]), low, high)
 
 
-def eye_pair():
+def eye_twice():
     row = lax.broadcasted_iota(jnp.int32, (64, 128), 0)
     lane = lax.broadcasted_iota(jnp.int32, (64, 128), 1)
-    return jnp.where((lane == row) | (lane == row + 64), 1.0, 0.0).astype(jnp.float32)
-
-
-def invert(starts):
+    return jnp.where(lane % 64 == row, 1.0, 0.0).astype(jnp.float32)
+
+
+def invert(pairs, parts):
+    lane = lax.broadcasted_iota(jnp.int32, (1, 128), 1)
+    spot = lane % 64
+    low8, low56 = low_lanes(8), low_lanes(56)
     row8 = lax.broadcasted_iota(jnp.int32, (8, 128), 0)
+    tail = lax.broadcasted_iota(jnp.int32, (64, 128), 1) % 64 >= 56
+
+    def spread(a, j, low):
+        first, second = a[:, j : j + 1], a[:, 64 + j : 65 + j]
+        return jnp.where(low, jnp.broadcast_to(first, a.shape), jnp.broadcast_to(second, a.shape))
 
     def eight_steps(top, rest):
-        for first in (0, 4):
-            tops = [jnp.broadcast_to(top[:, j : j + 1], (8, 128)) for j in range(first, first + 4)]
-            rests = [jnp.broadcast_to(rest[:, j : j + 1], (56, 128)) for j in range(first, first + 4)]
-            for step in range(4):
-                k = first + step
-                hit = row8 == k
-                scale = 1.0 / tops[step][k : k + 1, :]
-                line = top[k : k + 1, :] * scale
-                top = jnp.where(hit, line, top - tops[step] * line)
-                rest = rest - rests[step] * line
-                for j in range(step + 1, 4):
-                    part = tops[j][k : k + 1, :] * scale
-                    tops[j] = jnp.where(hit, part, tops[j] - tops[step] * part)
-                    rests[j] = rests[j] - rests[step] * part
-        whole = pltpu.roll(jnp.concatenate([rest, top], axis=0), 120, 1)
+        tops = [spread(top, j, low8) for j in range(8)]
+        if parts:
+            left = jnp.where(lane < 8, rest, pltpu.roll(rest, 72, 1))
+            high = left.astype(jnp.bfloat16).astype(jnp.float32)
+            low = pltpu.roll(left - high, 16, 1)
+            left = jnp.where(lane < 16, high, jnp.where(lane < 32, low, pltpu.roll(high, 32, 1)))
+            left = left[:, :48].astype(jnp.bfloat16)
+        else:
+            left = [spread(rest, j, low56) for j in range(8)]
+        for k in range(8):
+            hit = row8 == k
+            here = spot == k
+            scale = 1.0 / tops[k][k : k + 1, :]
+            line = jnp.where(here, scale, top[k : k + 1, :] * scale)
+            top = jnp.where(hit, line, jnp.where(here, 0.0, top) - tops[k] * line)
+            for j in range(k + 1, 8):
+                part = tops[j][k : k + 1, :] * scale
+                tops[j] = jnp.where(hit, part, tops[j] - tops[k] * part)
+        rest = jnp.where(spot < 8, 0.0, rest)
+        if parts:
+            lines = jnp.concatenate([jnp.where(low8, top, 0.0), jnp.where(low8, 0.0, top)], axis=0)
+            high, low = split(lines)
+            rest = rest - dot(left, jnp.concatenate([high, high, low], axis=0))
+        else:
+            for k in range(8):
+                rest = rest - left[k] * top[k : k + 1, :]
+        whole = jnp.concatenate([rest, top], axis=0)
+        whole = jnp.where(tail, pltpu.roll(whole, 56, 1), pltpu.roll(whole, 120, 1))
         return whole[0:8], whole[8:64]
 
     def body(_, carry):
         return tuple(eight_steps(*one) for one in carry)
 
-    done = lax.fori_loop(0, 8, body, tuple((start[0:8], start[8:64]) for start in starts))
-    wholes = [jnp.concatenate(one, axis=0) for one in done]
-    return [pick(whole, swap(whole)) for whole in wholes]
+    done = lax.fori_loop(0, 8, body, tuple((pair[0:8], pair[8:64]) for pair in pairs))
+    return [part for one in done for part in both(jnp.concatenate(one, axis=0))]
+
+
+def eye_less(product):
+    return eye_twice() - product
 
 
 def both(a):
@@ -82,14 +106,10 @@
     return pick(a, turned), pick(turned, a)
 
 
-def eye_less(product):
-    return eye_pair() - jnp.where(low_lanes(64), product, 0.0)
-
-
 def solve_kernel(
     len_ref, ranks_in, diag_in, v_ref, u_ref, b_ref,
     sum_ref, left_ref, right_ref,
-    ranks_ref, diag_ref, uall_ref, vall, lhs, stage, pair, chip, zbuf, ubuf, bbuf, agsrc, couple, first_t, second_t, early, late,
+    ranks_ref, diag_ref, uall_ref, vall, lhs, stage, pair, chip, zbuf, ubuf, bbuf, agsrc, couple, first_t, second_t, early, late, front_ref,
     loc_sem, v_s, v_r, u_s, u_r, d_s, d_r, z_s, z_r, h_s, h_r, b_s, b_r, e_s, e_r, ag_s, ag_r, ad_s, ad_r,
 ):
     x = lax.axis_index("node")
@@ -275,14 +295,15 @@
     send_z(2)
     send_plane(0)
     send_plane(1)
-    share(0)
     send_plane(2)
     for l in range(LEVELS):
         send_direct(u_direct, l)
+    share(0)
     share_copies[0].wait_recv()
 
     zero = [[both(part) for part in gathered(0, at)] for at in range(4)]
-    inverse = invert([eye_less(mm(panel[0], panel[1])) for panel, _ in zero])
+    minus = [eye_less(mm(panel[0], panel[1])) for panel, _ in zero]
+    inverse = invert([pick(minus[0], minus[1]), pick(minus[2], minus[3])], True)
     share(1)
     t_low, t_high = [], []
     for at in range(4):
@@ -291,6 +312,7 @@
         t_high.append(q_low - mm(t_low[at], g_low))
         first_t[at, 0] = t_low[at][0:128]
         first_t[at, 1] = t_high[at][0:128]
+    pass_on(u_direct, u_onward, 0)
     share_copies[1].wait_recv()
 
     def after_zero(l, at):
@@ -310,9 +332,9 @@
     ]
     start_all(early_copies)
     early[h, z] = agsrc[x, block]
-    inverse = invert([eye_less(mm(w1[at][0:64], w1[at + 1][0:64])) for at in (0, 2)])
+    minus = [eye_less(mm(w1[at][0:64], w1[at + 1][0:64])) for at in (0, 2)]
+    inverse = invert([pick(minus[0], minus[1])], False)
     share(2)
-    pass_on(u_direct, u_onward, 0)
     t1 = []
     for even in (0, 2):
         low, high = w1[even], w1[even + 1]
@@ -323,6 +345,8 @@
         couple[even // 2, 2] = inverse[even // 2]
     for at in range(4):
         second_t[at] = t1[at][0:64]
+    pass_on(u_direct, u_onward, 1)
+    pass_on(u_direct, u_onward, 2)
     share_copies[2].wait_recv()
 
     w2 = [after_zero(2, at) for at in range(4)]
@@ -335,9 +359,7 @@
         remote(late.at[h * 8 + z], late.at[h * 8 + z], ag_s.at[1], ag_r.at[1], core_peer(d)) for d in range(1, 16)
     ]
     start_all(late_copies)
-    pass_on(u_direct, u_onward, 1)
-    pass_on(u_direct, u_onward, 2)
-    (inverse,) = invert([eye_less(mm(own[0:64], sib[0:64]))])
+    inverse = invert([eye_less(mm(own[0:64], sib[0:64]))], False)[0]
     wait_all(early.at[h, 0:7], ag_r.at[0])
     early_share = remote(early.at[h], early.at[h], ad_s.at[0], ad_r.at[0], partner)
     go(early_share)
@@ -349,14 +371,6 @@
     c_0 = mm(inverse, a_02) - mm(c_1, a_01)
     last_01 = -pick(c_0, c_1)
     last_2 = inverse[:, :64]
-    early_share.wait_recv()
-    t_0 = early[:, :, 0:24].reshape(COLS, 128)
-    q_even, q_odd = both(early[:, :, 24:48].reshape(COLS, 128))
-    t_even = mm(q_odd - mm(q_even, couple[x // 2, 1]), couple[x // 2, 2])
-    t_odd = q_even - mm(t_even, couple[x // 2, 0])
-    t_1 = jnp.where(x % 2 == 0, t_even, t_odd)
-    t_0 = t_0 - mm(t_1, a_01)
-    front_high, front_low = split(pick(t_0, t_1))
     last_high, last_low = split(jnp.concatenate([last_01, last_2], axis=1))
     for l in range(LEVELS):
         for copy in u_onward[l]:
@@ -371,8 +385,23 @@
         right_ref[0:64, span] = last_h
         right_ref[64:128, span] = last_h
         right_ref[128:192, span] = last_l
-        front = dot(front_high, panel_high[0:128]) + (
-            dot(front_low, panel_high[0:128]) + dot(front_high, panel_low[0:128])
+        front_ref[0:128, span] = panel_high[0:128]
+        front_ref[128:256, span] = panel_low[0:128]
+
+    early_share.wait_recv()
+    t_0 = early[:, :, 0:24].reshape(COLS, 128)
+    q_even, q_odd = both(early[:, :, 24:48].reshape(COLS, 128))
+    t_even = mm(q_odd - mm(q_even, couple[x // 2, 1]), couple[x // 2, 2])
+    t_odd = q_even - mm(t_even, couple[x // 2, 0])
+    t_1 = jnp.where(x % 2 == 0, t_even, t_odd)
+    t_0 = t_0 - mm(t_1, a_01)
+    front_high, front_low = split(pick(t_0, t_1))
+    front_left = jnp.concatenate([front_high, front_low], axis=1)
+    for part in range(4):
+        span = slice(512 * part, 512 * part + 512)
+        panel_high = front_ref[0:128, span]
+        front = dot(front_left, jnp.concatenate([panel_high, panel_high], axis=0)) + dot(
+            front_high, front_ref[128:256, span]
         )
         sum_ref[:, span] = lhs[0:COLS, span].astype(jnp.float32) * over[:, span] - front * weight[:, span]
 
@@ -431,6 +460,7 @@
             pltpu.VMEM((4, 64, 128), f32),
             pltpu.VMEM((2, 8, 48, 128), f32),
             pltpu.VMEM((16, 24, 128), f32),
+            pltpu.VMEM((256, ROWS), jnp.bfloat16),
             dma((5,)),
             dma((LEVELS, 4)), dma((LEVELS, 4)),
             dma((LEVELS, 4)), dma((LEVELS, 4)),
@@ -458,7 +488,7 @@
             )
         ]
     )
-    width = 512
+    width = 1024
     return pl.pallas_call(
         functools.partial(final_kernel, width),
         name="add_last_panel",

time: 63.7 us -> 60.3 us (0.947)
  Pallas kernels: 62.9 us -> 59.6 us
    pallas_call x1, Pallas kernels: 60.3 us -> 57.5 us  [local(): pl.pallas_call(solve_kernel, name='gather_and_solve', out_shape=(pltpu.VM...]
where the time goes in v4:
time: 60.3 us; the launch traced here: 60.2 us
  Pallas kernels  59.6 us (99%)
  between operations  0.66 us (1%)
    pallas_call x1, Pallas kernels, local(): pl.pallas_call(solve_kernel, name='gather_and_solve', out_shape=(pltpu.VM...  57.5 us
    pallas_call x1, Pallas kernels, local(): pl.pallas_call(functools.partial(final_kernel, width), name='add_last_pan...  2.05 us

profile of v4, /device:TPU:1, one launch (start us, length us, event | category | flops | bytes accessed | tf_op | source)
XLA Modules:
  0.0 60.2 jit_solution(18326752899026159147)
XLA Ops:
  0.7 57.5 %gather_and_solve.1 = (f32[384,2048]{1,0:T(8,128)S(1)}, bf16[384,192]{1,0:T(8,128)(2,1)S(1)}, bf16[192,2048]{1,0:T(8,128)(2,1)S(1)}) custom-call(s32[1]{0:T(128)S(6)} %copy.7.len_ref, s32[3]{0:T(128)} %ranks_in.1, f32[1,2048]{1,0:T(1,128)} %bitcast.5, f32[3,2,8,2048]{3,2,1,0:T(8,128)} %bitcast.3, f32[3,2,8,2048]{3,2,1,0:T(8,128)} %bitcast.4, ...), custom_call_target="tpu_custom_call" | custom-call | tf_op jit(solution)/shard_map/gather_and_solve/pallas_call | solution.py:435
  58.2 2.0 %add_last_panel.1 = f32[384,2048]{1,0:T(8,128)} custom-call(f32[384,2048]{1,0:T(8,128)S(1)} %get-tuple-element.8.sum_ref, bf16[384,192]{1,0:T(8,128)(2,1)S(1)} %get-tuple-element.9.left_ref, bf16[192,2048]{1,0:T(8,128)(2,1)S(1)} %get-tuple-element.10.right_ref), custom_call_target="tpu_custom_call" | custom-call | flops 301989888 | bytes 7200000 | tf_op jit(solution)/shard_map/add_last_panel/pallas_call | solution.py:492

commit v5 on v4

--- a/solution.py
+++ b/solution.py
@@ -109,7 +109,7 @@
 def solve_kernel(
     len_ref, ranks_in, diag_in, v_ref, u_ref, b_ref,
     sum_ref, left_ref, right_ref,
-    ranks_ref, diag_ref, uall_ref, vall, lhs, stage, pair, chip, zbuf, ubuf, bbuf, agsrc, couple, first_t, second_t, early, late, front_ref,
+    ranks_ref, diag_ref, uall_ref, vall, lhs, stage, pair, chip, zbuf, ubuf, bbuf, agsrc, couple, first_t, second_t, early, late, front_ref, ready,
     loc_sem, v_s, v_r, u_s, u_r, d_s, d_r, z_s, z_r, h_s, h_r, b_s, b_r, e_s, e_r, ag_s, ag_r, ad_s, ad_r,
 ):
     x = lax.axis_index("node")
@@ -142,7 +142,15 @@
     def plane_peer(d):
         return ((x + d // 4) % 4, row, (y + d % 4) % 4)
 
-    peers = [core_peer(d) for d in range(1, 16)] + [plane_peer(d) for d in range(1, 16)]
+    peers = [partner, z_peer(1), z_peer(7)] + [plane_peer(d) for d in (1, 3, 4, 12)]
+
+    def tell(i):
+        for peer in peers:
+            pl.semaphore_signal(ready.at[i], inc=1, device_id=peer, device_id_type=MESH)
+
+    def hear(i):
+        pl.semaphore_wait(ready.at[i], len(peers))
+
     barrier = pltpu.get_barrier_semaphore()
     for peer in peers:
         pl.semaphore_signal(barrier, inc=1, device_id=peer, device_id_type=MESH)
@@ -210,6 +218,7 @@
 
     send_direct(v_direct, 0)
     send_direct(v_direct, 1)
+    tell(0)
     own_v.wait()
     own_b.wait()
 
@@ -282,10 +291,16 @@
 
     pass_on(v_direct, v_onward, 0)
     send_direct(v_direct, 2)
+    hear(0)
+    tell(1)
     pass_on(v_direct, v_onward, 1)
+    hear(1)
+    tell(2)
     product(0)
     go(d_copies[0])
+    hear(2)
     send_z(0)
+    tell(3)
     pass_on(v_direct, v_onward, 2)
     product(1)
     go(d_copies[1])
@@ -358,6 +373,7 @@
     late_copies = [
         remote(late.at[h * 8 + z], late.at[h * 8 + z], ag_s.at[1], ag_r.at[1], core_peer(d)) for d in range(1, 16)
     ]
+    hear(3)
     start_all(late_copies)
     inverse = invert([eye_less(mm(own[0:64], sib[0:64]))], False)[0]
     wait_all(early.at[h, 0:7], ag_r.at[0])
@@ -461,6 +477,7 @@
             pltpu.VMEM((2, 8, 48, 128), f32),
             pltpu.VMEM((16, 24, 128), f32),
             pltpu.VMEM((256, ROWS), jnp.bfloat16),
+            pltpu.SemaphoreType.REGULAR((4,)),
             dma((5,)),
             dma((LEVELS, 4)), dma((LEVELS, 4)),
             dma((LEVELS, 4)), dma((LEVELS, 4)),

time: 60.3 us -> 58.1 us (0.964)
  Pallas kernels: 59.6 us -> 57.4 us
    pallas_call x1, Pallas kernels: 57.5 us -> 55.3 us  [local(): pl.pallas_call(solve_kernel, name='gather_and_solve', out_shape=(pltpu.VM...]
where the time goes in v5:
time: 58.1 us; the launch traced here: 58 us
  Pallas kernels  57.4 us (99%)
  between operations  0.66 us (1%)
    pallas_call x1, Pallas kernels, local(): pl.pallas_call(solve_kernel, name='gather_and_solve', out_shape=(pltpu.VM...  55.3 us
    pallas_call x1, Pallas kernels, local(): pl.pallas_call(functools.partial(final_kernel, width), name='add_last_pan...  2.05 us

profile of v5, /device:TPU:1, one launch (start us, length us, event | category | flops | bytes accessed | tf_op | source)
XLA Modules:
  0.0 58.0 jit_solution(1191683808223074766)
XLA Ops:
  0.7 55.3 %gather_and_solve.1 = (f32[384,2048]{1,0:T(8,128)S(1)}, bf16[384,192]{1,0:T(8,128)(2,1)S(1)}, bf16[192,2048]{1,0:T(8,128)(2,1)S(1)}) custom-call(s32[1]{0:T(128)S(6)} %copy.7.len_ref, s32[3]{0:T(128)} %ranks_in.1, f32[1,2048]{1,0:T(1,128)} %bitcast.5, f32[3,2,8,2048]{3,2,1,0:T(8,128)} %bitcast.3, f32[3,2,8,2048]{3,2,1,0:T(8,128)} %bitcast.4, ...), custom_call_target="tpu_custom_call" | custom-call | tf_op jit(solution)/shard_map/gather_and_solve/pallas_call | solution.py:451
  56.0 2.1 %add_last_panel.1 = f32[384,2048]{1,0:T(8,128)} custom-call(f32[384,2048]{1,0:T(8,128)S(1)} %get-tuple-element.8.sum_ref, bf16[384,192]{1,0:T(8,128)(2,1)S(1)} %get-tuple-element.9.left_ref, bf16[192,2048]{1,0:T(8,128)(2,1)S(1)} %get-tuple-element.10.right_ref), custom_call_target="tpu_custom_call" | custom-call | flops 301989888 | bytes 7200000 | tf_op jit(solution)/shard_map/add_last_panel/pallas_call | solution.py:509

commit v6 on v5

--- a/solution.py
+++ b/solution.py
@@ -11,6 +11,9 @@
 ROWS = 2048
 COLS = 384
 MESH = pl.DeviceIdType.MESH
+FAR_Z = (4, 3, 5, 2, 6, 1, 7)
+FAR_CORE = (8, 7, 9, 6, 10, 5, 11, 4, 12, 3, 13, 2, 14, 1, 15)
+FAR_PLANE = (10, 6, 14, 9, 11, 2, 8, 5, 7, 13, 15, 1, 3, 4, 12)
 
 
 def split(a):
@@ -246,12 +249,12 @@
 
     d_copies = [remote(stage.at[l, 1 - h], pair.at[l], d_s.at[l], d_r.at[l], partner) for l in range(LEVELS)]
     z_copies = [
-        [remote(chip.at[l, (z + d) % 8], zbuf.at[l, z], z_s.at[l], z_r.at[l], z_peer(d)) for d in range(1, 8)]
+        [remote(chip.at[l, (z + d) % 8], zbuf.at[l, z], z_s.at[l], z_r.at[l], z_peer(d)) for d in FAR_Z]
         for l in range(LEVELS)
     ]
     spot = x * 4 + y
     u_copies = [
-        [remote(ubuf.at[l, h, spot], ubuf.at[l, h, spot], h_s.at[l], h_r.at[l], plane_peer(d)) for d in range(1, 16)]
+        [remote(ubuf.at[l, h, spot], ubuf.at[l, h, spot], h_s.at[l], h_r.at[l], plane_peer(d)) for d in FAR_PLANE]
         for l in range(LEVELS)
     ]
     b_copies = [
@@ -311,9 +314,9 @@
     send_plane(0)
     send_plane(1)
     send_plane(2)
+    share(0)
     for l in range(LEVELS):
         send_direct(u_direct, l)
-    share(0)
     share_copies[0].wait_recv()
 
     zero = [[both(part) for part in gathered(0, at)] for at in range(4)]
@@ -343,7 +346,7 @@
             agsrc[at, c, 24:48] = sides
     early_copies = [
         remote(agsrc.at[x, ((z + d) % 8) // 4], early.at[h, z], ag_s.at[0], ag_r.at[0], z_peer(d))
-        for d in range(1, 8)
+        for d in FAR_Z
     ]
     start_all(early_copies)
     early[h, z] = agsrc[x, block]
@@ -371,7 +374,7 @@
     sib = jnp.where(x < 2, high, low)
     late[h * 8 + z] = pick(own[64:88], sib[64:88])
     late_copies = [
-        remote(late.at[h * 8 + z], late.at[h * 8 + z], ag_s.at[1], ag_r.at[1], core_peer(d)) for d in range(1, 16)
+        remote(late.at[h * 8 + z], late.at[h * 8 + z], ag_s.at[1], ag_r.at[1], core_peer(d)) for d in FAR_CORE
     ]
     hear(3)
     start_all(late_copies)

time: 58.1 us -> 57.3 us (0.986)
  Pallas kernels: 57.4 us -> 56.5 us
    pallas_call x1, Pallas kernels: 55.3 us -> 54.5 us  [local(): pl.pallas_call(solve_kernel, name='gather_and_solve', out_shape=(pltpu.VM...]
where the time goes in v6:
time: 57.3 us; the launch traced here: 57.2 us
  Pallas kernels  56.5 us (99%)
  between operations  0.66 us (1%)
    pallas_call x1, Pallas kernels, local(): pl.pallas_call(solve_kernel, name='gather_and_solve', out_shape=(pltpu.VM...  54.5 us
    pallas_call x1, Pallas kernels, local(): pl.pallas_call(functools.partial(final_kernel, width), name='add_last_pan...  2.05 us

profile of v6, /device:TPU:1, one launch (start us, length us, event | category | flops | bytes accessed | tf_op | source)
XLA Modules:
  0.0 57.2 jit_solution(1009186412406123271)
XLA Ops:
  0.7 54.5 %gather_and_solve.1 = (f32[384,2048]{1,0:T(8,128)S(1)}, bf16[384,192]{1,0:T(8,128)(2,1)S(1)}, bf16[192,2048]{1,0:T(8,128)(2,1)S(1)}) custom-call(s32[1]{0:T(128)S(6)} %copy.7.len_ref, s32[3]{0:T(128)} %ranks_in.1, f32[1,2048]{1,0:T(1,128)} %bitcast.5, f32[3,2,8,2048]{3,2,1,0:T(8,128)} %bitcast.3, f32[3,2,8,2048]{3,2,1,0:T(8,128)} %bitcast.4, ...), custom_call_target="tpu_custom_call" | custom-call | tf_op jit(solution)/shard_map/gather_and_solve/pallas_call | solution.py:454
  55.1 2.0 %add_last_panel.1 = f32[384,2048]{1,0:T(8,128)} custom-call(f32[384,2048]{1,0:T(8,128)S(1)} %get-tuple-element.8.sum_ref, bf16[384,192]{1,0:T(8,128)(2,1)S(1)} %get-tuple-element.9.left_ref, bf16[192,2048]{1,0:T(8,128)(2,1)S(1)} %get-tuple-element.10.right_ref), custom_call_target="tpu_custom_call" | custom-call | flops 301989888 | bytes 7200000 | tf_op jit(solution)/shard_map/add_last_panel/pallas_call | solution.py:512

commit v7 on v6

--- a/solution.py
+++ b/solution.py
@@ -364,7 +364,6 @@
     for at in range(4):
         second_t[at] = t1[at][0:64]
     pass_on(u_direct, u_onward, 1)
-    pass_on(u_direct, u_onward, 2)
     share_copies[2].wait_recv()
 
     w2 = [after_zero(2, at) for at in range(4)]
@@ -378,6 +377,7 @@
     ]
     hear(3)
     start_all(late_copies)
+    pass_on(u_direct, u_onward, 2)
     inverse = invert([eye_less(mm(own[0:64], sib[0:64]))], False)[0]
     wait_all(early.at[h, 0:7], ag_r.at[0])
     early_share = remote(early.at[h], early.at[h], ad_s.at[0], ad_r.at[0], partner)

time: 57.3 us -> 57.2 us (level)
  no operation moved by 1% of the time
where the time goes in v7:
time: 57.2 us; the launch traced here: 57 us
  Pallas kernels  56.4 us (99%)
  between operations  0.66 us (1%)
    pallas_call x1, Pallas kernels, local(): pl.pallas_call(solve_kernel, name='gather_and_solve', out_shape=(pltpu.VM...  54.3 us
    pallas_call x1, Pallas kernels, local(): pl.pallas_call(functools.partial(final_kernel, width), name='add_last_pan...  2.05 us

profile of v7, /device:TPU:1, one launch (start us, length us, event | category | flops | bytes accessed | tf_op | source)
XLA Modules:
  0.0 57.0 jit_solution(1204469469332553680)
XLA Ops:
  0.7 54.3 %gather_and_solve.1 = (f32[384,2048]{1,0:T(8,128)S(1)}, bf16[384,192]{1,0:T(8,128)(2,1)S(1)}, bf16[192,2048]{1,0:T(8,128)(2,1)S(1)}) custom-call(s32[1]{0:T(128)S(6)} %copy.7.len_ref, s32[3]{0:T(128)} %ranks_in.1, f32[1,2048]{1,0:T(1,128)} %bitcast.5, f32[3,2,8,2048]{3,2,1,0:T(8,128)} %bitcast.3, f32[3,2,8,2048]{3,2,1,0:T(8,128)} %bitcast.4, ...), custom_call_target="tpu_custom_call" | custom-call | tf_op jit(solution)/shard_map/gather_and_solve/pallas_call | solution.py:454
  55.0 2.0 %add_last_panel.1 = f32[384,2048]{1,0:T(8,128)} custom-call(f32[384,2048]{1,0:T(8,128)S(1)} %get-tuple-element.8.sum_ref, bf16[384,192]{1,0:T(8,128)(2,1)S(1)} %get-tuple-element.9.left_ref, bf16[192,2048]{1,0:T(8,128)(2,1)S(1)} %get-tuple-element.10.right_ref), custom_call_target="tpu_custom_call" | custom-call | flops 301989888 | bytes 7200000 | tf_op jit(solution)/shard_map/add_last_panel/pallas_call | solution.py:512
